TPU v7x, 256 devices: a whole 4x4x8 slice. The times are simulated.
256 devices in a mesh: depth: 8 (over y, core), cols: 32 (over z, x).
Axes of the slice: x: 4, y: 4, z: 8, core: 2. Of those that a mesh axis runs over, the one named last changes fastest.
Arguments:
- density: bfloat16 [1024, 4096, 128], P('depth', 'cols'), may hold values from -6 to 6
- occupancy: int32 [64, 256, 4], P('depth', 'cols'), may hold values from 0 to 1, as said below
- light_dir: float32 [3], replicated, may hold values from -4 to 4
- palette: float32 [4, 2], replicated, may hold values from 0.5 to 2
Outputs:
- final_image: float32 [4, 4096, 128], P(None, None, 'depth')
Inputs may be any that keep to these rules, and one draw needn't show every extreme that they name: `occupancy`: 1 marks an occupied block of 16 x 16 x 32 cells; the share of occupied blocks differs from one depth layer of blocks to another.
All inputs are finite; a program needn't handle non-finite values.
Results may differ from a plain program's by a relative error of at most 0.0003.
Values may be sent and summed in bfloat16 or wider, within the bound.
No kernel may reach another device: no remote copies, remote signals or barrier semaphores. Data moves between devices by JAX's collectives and lax.ppermute only.
A program may use at most 192 MiB of HBM per device.

v0:
```python
import jax
import jax.numpy as jnp
from jax import lax
from jax.sharding import PartitionSpec as P


def with_halo(value, sides, width):
    for axis, dim in sides:
        size, length = (lax.axis_size(axis), value.shape[dim])
        up = [(i, (i + 1) % size) for i in range(size - 1)]
        down = [(j, i) for i, j in up]
        last = lax.slice_in_dim(value, length - width, length, axis=dim)
        initial = lax.slice_in_dim(value, 0, width, axis=dim)
        before = lax.ppermute(last, axis, up)
        after = lax.ppermute(initial, axis, down)
        value = jnp.concatenate([before, value, after], axis=dim)
    return value


def from_partner(block, axis, distance):
    count = lax.axis_size(axis)
    route = []
    for low in range(count):
        high = low | 1 << distance
        if high != low and high < count:
            route += [(low, high), (high, low)]
    return lax.ppermute(block, axis, route)


def expand_cells(values, occ):
    mz, mx, my = occ.shape
    planes, columns, rows = values.shape
    shaped = values.reshape(mz, planes // mz, mx, columns // mx, my, rows // my)
    return (shaped * occ.astype(jnp.float32)[:, None, :, None, :, None]).reshape(
        planes, columns, rows
    )


def composite_pair(front_part, back_part):
    colours = front_part[:3] + jnp.exp(-front_part[3:]) * back_part[:3]
    return jnp.concatenate([colours, front_part[3:] + back_part[3:]], axis=0)


def local(density, occupancy, light_dir, palette):
    planes, columns, rows = density.shape
    slabs = lax.axis_size("depth")
    padded = with_halo(density, (("depth", 0), ("cols", 1)), 1)
    values = padded.astype(jnp.float32)
    centre = values[1:-1, 1:-1, :]
    grad_z = 0.5 * (values[2:, 1:-1, :] - values[:-2, 1:-1, :])
    grad_x = 0.5 * (values[1:-1, 2:, :] - values[1:-1, :-2, :])
    row_padded = jnp.pad(centre, ((0, 0), (0, 0), (1, 1)))
    grad_y = 0.5 * (row_padded[:, :, 2:] - row_padded[:, :, :-2])
    factor = 1.0 / jnp.sqrt(1.0 + grad_z * grad_z + grad_x * grad_x + grad_y * grad_y)
    facing = (grad_z * light_dir[0] + grad_x * light_dir[1] + grad_y * light_dir[2]) * factor
    shading = 0.3 + 0.7 * jnp.tanh(jnp.abs(facing))
    optical = 3.0 / (planes * slabs) * jax.nn.softplus(palette[3, 0] * centre + palette[3, 1])
    optical = expand_cells(optical, occupancy)
    row_index = lax.broadcasted_iota(jnp.int32, (planes, planes), 0)
    col_index = lax.broadcasted_iota(jnp.int32, (planes, planes), 1)
    in_front = (col_index > row_index).astype(jnp.float32)
    ahead_depth = jnp.dot(
        in_front, optical.reshape(planes, columns * rows), precision=lax.Precision.HIGHEST
    ).reshape(planes, columns, rows)
    weight = (1.0 - jnp.exp(-optical)) * jnp.exp(-ahead_depth) * shading
    channels = [
        jnp.sum(jax.nn.sigmoid(palette[c, 0] * centre + palette[c, 1]) * weight, axis=0)
        for c in range(3)
    ]
    channels.append(jnp.sum(optical, axis=0))
    partial_image = jnp.stack(channels, axis=0)
    depth_index = lax.axis_index("depth")
    levels = slabs.bit_length() - 1
    block_rows = rows // slabs
    image = partial_image.reshape(4, columns, slabs, block_rows)
    for bit_number in range(levels):
        remaining = image.shape[2]
        paired = image.reshape(4, columns, remaining // 2, 2, block_rows)
        lower_half = paired[:, :, :, 0]
        upper_half = paired[:, :, :, 1]
        my_bit = depth_index >> bit_number & 1
        kept_half = jnp.where(my_bit == 1, upper_half, lower_half)
        sent_half = jnp.where(my_bit == 1, lower_half, upper_half)
        their_half = from_partner(sent_half, "depth", bit_number)
        mine_front = my_bit == 1
        front_part = jnp.where(mine_front, kept_half, their_half)
        back_part = jnp.where(mine_front, their_half, kept_half)
        image = composite_pair(front_part, back_part)
    image = image.reshape(4, columns, block_rows)
    pixels = jnp.concatenate([image[:3], 1.0 - jnp.exp(-image[3:])], axis=0)
    return lax.all_gather(pixels, "cols", axis=1, tiled=True)


def solution(mesh):
    placed = (P("depth", "cols", None), P("depth", "cols", None), P(), P())
    return jax.shard_map(
        local, mesh=mesh, in_specs=placed, out_specs=P(None, None, "depth"), check_vma=False
    )
```

profile of v0, /device:TPU:2, one launch (start us, length us, event | category | flops | bytes accessed | tf_op | source)
XLA Modules:
  0.0 288.6 jit_solution(8927103453942306292)
XLA Ops:
  6.5 0.0 copy-start.3
  6.5 0.0 copy-start.4
  6.5 0.0 copy-start.2
  6.5 0.0 all-gather.2.cloned.1.call-start
  6.5 4.9 %copy.30 = bf16[128,128,128]{2,0,1:T(8,128)(2,1)S(1)} copy(bf16[128,128,128]{2,1,0:T(8,128)(2,1)} %param.4) | data formatting | bytes 8388608 | tf_op args[0]
  11.5 0.0 copy-start
  11.5 0.1 fusion.17
  11.6 1.7 collective-permute-start
  13.3 1.3 collective-permute-start.1
  14.6 0.0 copy-done.3
  14.7 0.7 fusion.18
  15.3 0.0 collective-permute-done
  15.3 2.5 collective-permute-done.1
  17.9 0.0 copy-done
  17.9 3.4 %collective-permute-start.2 = (bf16[130,1,128]{2,0,1:T(8,128)(2,1)S(1)}, bf16[130,1,128]{2,0,1:T(8,128)(2,1)S(1)}, u32[]{:S(2)}, u32[]{:S(2)}) collective-permute-start(bf16[130,1,128]{2,0,1:T(8,128)(2,1)S(1)} %get-tuple-element.11), channel_id=1, source_target_pairs={{0,1},{1,2},{2,3},{3,4},{4,5},{5,6},{6,7},{7,8},{8,9},{9,10},{10,1... | collective-permute-start | bytes 99848 | tf_op jit(solution)/shard_map/ppermute | solution.py:14
  21.3 2.6 collective-permute-start.3
  23.9 0.0 copy-done.4
  23.9 0.7 fusion.19
  24.6 0.0 copy-done.2
  24.6 0.1 copy.33
  24.7 11.3 %mul.154 = f32[8,16,8,16,4,32]{5,4,3,2,1,0:T(4,128)} broadcast(f32[8,8,4]{2,1,0:T(8,128)S(1)} %copy.33), dimensions={0,2,4} | broadcast | bytes 8389632 | tf_op jit(solution)/shard_map/mul | solution.py:34
  36.0 25.7 %reshape.115 = f32[128,128,128]{2,1,0:T(8,128)} reshape(f32[8,16,8,16,4,32]{5,4,3,2,1,0:T(4,128)} %mul.154) | data formatting | bytes 16777216 | tf_op jit(solution)/shard_map/mul | solution.py:34
  61.7 32.5 %mul.157 = f32[128,16384]{1,0:T(8,128)} reshape(f32[8,16,8,16,4,32]{5,4,3,2,1,0:T(4,128)} %mul.154) | data formatting | bytes 16777216 | tf_op jit(solution)/shard_map/mul | solution.py:34
  96.3 9.0 %copy.36 = f32[128,16384]{0,1:T(8,128)} copy(f32[128,16384]{1,0:T(8,128)} %mul.157) | data formatting | bytes 16777216 | tf_op jit(solution)/shard_map/mul | solution.py:34
  105.3 0.0 collective-permute-done.2
  105.3 0.0 collective-permute-done.3
  105.3 4.9 %maximum_convert_fusion = f32[130,130,128]{2,0,1:T(8,128)S(1)} fusion(bf16[130,1,128]{2,0,1:T(8,128)(2,1)S(1)} %collective-permute-done.3, bf16[1,128,128]{2,0,1:T(2,128)(2,1)S(1)} %collective-permute-done.1, bf16[128,128,128]{2,0,1:T(8,128)(2,1)} %copy-done, bf16[1,128,128]{2,0,1:T(2,128)(2,1)S(1)} %collective-permute-done, ...), kind=kLoop, calls=%fused_computation.13 | loop fusion | flops 21632000 | bytes 12979200 | tf_op jit(solution)/shard_map/convert_element_type | solution.py:48
  110.2 0.0 copy-start.1
  110.2 17.9 %fusion.2 = (f32[128,128]{1,0:T(8,128)S(1)}, f32[128,128,128]{2,0,1:T(8,128)}, f32[128,128,128]{2,0,1:T(8,128)}) fusion(f32[128,128,128]{2,1,0:T(8,128)} %reshape.115, f32[]{:T(128)} %bitcast.3, f32[130,130,128]{2,0,1:T(8,128)S(1)} %maximum_convert_fusion, f32[]{:T(128)} %bitcast.2), kind=kLoop, calls=%fused_computation.14 | loop fusion | flops 23052288 | bytes 33619976 | tf_op jit(solution)/shard_map/reduce_sum | solution.py:70
  128.1 0.0 copy-done.1
  128.1 0.1 copy.40
  128.2 9.0 %copy.35 = f32[128,128,128]{0,2,1:T(8,128)} copy(f32[128,128,128]{2,0,1:T(8,128)} %get-tuple-element.9) | data formatting | bytes 16777216 | tf_op jit(solution)/shard_map/mul | solution.py:57
  137.2 9.8 %bitcast_multiply_fusion = f32[128,16384]{0,1:T(8,128)} fusion(f32[128,16384]{0,1:T(8,128)} %copy.36, f32[128,128,128]{0,2,1:T(8,128)} %copy.35), kind=kLoop, calls=%fused_computation.7 | loop fusion | flops 2097152 | bytes 25165824 | tf_op jit(solution)/shard_map/mul | solution.py:34
  147.0 43.2 %multiply_reduce_fusion.2 = (f32[128,128]{1,0:T(8,128)S(1)}, f32[128,128]{1,0:T(8,128)S(1)}, f32[128,128]{1,0:T(8,128)S(1)}) fusion(f32[]{:T(128)} %bitcast.1, f32[]{:T(128)} %bitcast, f32[130,130,128]{2,0,1:T(8,128)} %copy-done.1, f32[]{:T(128)} %bitcast.16, f32[]{:T(128)} %bitcast.15, f32[]{:T(128)} %bitcast.13, f32[]{:T(128)} %bitcast.12, f32[]{:T(128)} %bitcast.10, ...), kind=kOutput, calls=%fused_computation.11 | convolution fusion | flops 3321856000 | bytes 75694112 | tf_op jit(solution)/shard_map/dot_general | solution.py:62
  190.2 0.1 copy.37
  190.3 0.1 copy.39
  190.4 0.1 copy.38
  190.5 2.5 collective-permute-start.4
  193.0 1.0 collective-permute-done.4
  194.1 1.7 collective-permute-start.5
  195.8 2.8 collective-permute-done.5
  198.6 3.0 %collective-permute-start.6 = (f32[4,128,1,16]{1,3,0,2:T(8,128)S(1)}, f32[4,128,1,16]{1,3,0,2:T(8,128)S(1)}, u32[]{:S(2)}, u32[]{:S(2)}) collective-permute-start(f32[4,128,1,16]{1,3,0,2:T(8,128)S(1)} %select_bitcast_fusion.2), channel_id=1, source_target_pairs={{0,128},{128,0},{32,160},{160,32},{64,192},{192,64},{96,224},{224,... | collective-permute-start | bytes 98312 | tf_op jit(solution)/shard_map/ppermute | solution.py:27
  201.6 2.5 collective-permute-done.6
  204.2 0.6 pad_maximum_fusion.5
  204.8 0.0 all-gather.2.cloned.1.call-update
  204.8 74.7 %all-gather.2.cloned.1.call-done = f32[4,4096,16]{1,2,0:T(8,128)} async-done(((f32[4,128,16]{1,2,0:T(8,128)}), f32[4,4096,16]{1,2,0:T(8,128)}) %all-gather.2.cloned.1.call-update) | async-done | bytes 1048592 | tf_op jit(solution)/shard_map/all_gather | solution.py:91
  279.5 2.3 copy.63
  (17 shorter events, 0.2 us)
Async XLA Ops:
  6.5 8.1 %copy-start.3 = (f32[4,2]{0,1:T(2,128)S(1)}, f32[4,2]{0,1:T(2,128)}, u32[]{:S(2)}) copy-start(f32[4,2]{0,1:T(2,128)} %param.7) | copy-start | bytes 100
  6.5 17.4 %copy-start.4 = (f32[3]{0:T(128)S(1)}, f32[3]{0:T(128)}, u32[]{:S(2)}) copy-start(f32[3]{0:T(128)} %param.6) | copy-start | bytes 40
  6.5 18.1 %copy-start.2 = (s32[8,8,4]{1,2,0:T(4,128)S(1)}, s32[8,8,4]{1,2,0:T(4,128)}, u32[]{:S(2)}) copy-start(s32[8,8,4]{1,2,0:T(4,128)} %param.5) | copy-start | bytes 3076
  6.5 273.0 %all-gather.2.cloned.1.call-start = ((), (), s32[]{:S(2)}) async-start(), calls=%async_computation | async-start | bytes 1081344 | tf_op jit(solution)/shard_map/all_gather | solution.py:91
  11.5 6.4 %copy-start = (bf16[128,128,128]{2,0,1:T(8,128)(2,1)}, bf16[128,128,128]{2,0,1:T(8,128)(2,1)S(1)}, u32[]{:S(2)}) copy-start(bf16[128,128,128]{2,0,1:T(8,128)(2,1)S(1)} %copy.30) | copy-start | bytes 12582916
  11.6 3.7 %collective-permute-start = (bf16[1,128,128]{2,0,1:T(2,128)(2,1)S(1)}, bf16[1,128,128]{2,0,1:T(2,128)(2,1)S(1)}, u32[]{:S(2)}, u32[]{:S(2)}) collective-permute-start(bf16[1,128,128]{2,0,1:T(2,128)(2,1)S(1)} %get-tuple-element.13), channel_id=1, source_target_pairs={{0,32},{32,64},{64,96},{96,128},{128,160},{160,192},{192,224},{1,3... | collective-permute-start | bytes 98312 | tf_op jit(solution)/shard_map/ppermute | solution.py:14
  13.3 4.5 %collective-permute-start.1 = (bf16[1,128,128]{2,0,1:T(2,128)(2,1)S(1)}, bf16[1,128,128]{2,0,1:T(2,128)(2,1)S(1)}, u32[]{:S(2)}, u32[]{:S(2)}) collective-permute-start(bf16[1,128,128]{2,0,1:T(2,128)(2,1)S(1)} %get-tuple-element.14), channel_id=1, source_target_pairs={{32,0},{64,32},{96,64},{128,96},{160,128},{192,160},{224,192},{33,... | collective-permute-start | bytes 98312 | tf_op jit(solution)/shard_map/ppermute | solution.py:15
  17.9 87.4 %collective-permute-start.2 = (bf16[130,1,128]{2,0,1:T(8,128)(2,1)S(1)}, bf16[130,1,128]{2,0,1:T(8,128)(2,1)S(1)}, u32[]{:S(2)}, u32[]{:S(2)}) collective-permute-start(bf16[130,1,128]{2,0,1:T(8,128)(2,1)S(1)} %get-tuple-element.11), channel_id=1, source_target_pairs={{0,1},{1,2},{2,3},{3,4},{4,5},{5,6},{6,7},{7,8},{8,9},{9,10},{10,1... | collective-permute-start | bytes 99848 | tf_op jit(solution)/shard_map/ppermute | solution.py:14
  21.3 84.0 %collective-permute-start.3 = (bf16[130,1,128]{2,0,1:T(8,128)(2,1)S(1)}, bf16[130,1,128]{2,0,1:T(8,128)(2,1)S(1)}, u32[]{:S(2)}, u32[]{:S(2)}) collective-permute-start(bf16[130,1,128]{2,0,1:T(8,128)(2,1)S(1)} %get-tuple-element.12), channel_id=1, source_target_pairs={{1,0},{2,1},{3,2},{4,3},{5,4},{6,5},{7,6},{8,7},{9,8},{10,9},{11,1... | collective-permute-start | bytes 99848 | tf_op jit(solution)/shard_map/ppermute | solution.py:15
  110.2 17.9 %copy-start.1 = (f32[130,130,128]{2,0,1:T(8,128)}, f32[130,130,128]{2,0,1:T(8,128)S(1)}, u32[]{:S(2)}) copy-start(f32[130,130,128]{2,0,1:T(8,128)S(1)} %maximum_convert_fusion) | copy-start | bytes 25958404
  190.5 3.5 %collective-permute-start.4 = (f32[4,128,4,16]{1,3,2,0:T(8,128)S(1)}, f32[4,128,4,16]{1,3,2,0:T(8,128)S(1)}, u32[]{:S(2)}, u32[]{:S(2)}) collective-permute-start(f32[4,128,4,16]{1,3,2,0:T(8,128)S(1)} %select_bitcast_fusion), channel_id=1, source_target_pairs={{0,32},{32,0},{64,96},{96,64},{128,160},{160,128},{192,224},{224,1... | collective-permute-start | bytes 393224 | tf_op jit(solution)/shard_map/ppermute | solution.py:27
  194.1 4.4 %collective-permute-start.5 = (f32[4,128,2,16]{1,3,2,0:T(8,128)S(1)}, f32[4,128,2,16]{1,3,2,0:T(8,128)S(1)}, u32[]{:S(2)}, u32[]{:S(2)}) collective-permute-start(f32[4,128,2,16]{1,3,2,0:T(8,128)S(1)} %select_bitcast_fusion.1), channel_id=1, source_target_pairs={{0,64},{64,0},{32,96},{96,32},{128,192},{192,128},{160,224},{224,1... | collective-permute-start | bytes 196616 | tf_op jit(solution)/shard_map/ppermute | solution.py:27
  198.6 5.5 %collective-permute-start.6 = (f32[4,128,1,16]{1,3,0,2:T(8,128)S(1)}, f32[4,128,1,16]{1,3,0,2:T(8,128)S(1)}, u32[]{:S(2)}, u32[]{:S(2)}) collective-permute-start(f32[4,128,1,16]{1,3,0,2:T(8,128)S(1)} %select_bitcast_fusion.2), channel_id=1, source_target_pairs={{0,128},{128,0},{32,160},{160,32},{64,192},{192,64},{96,224},{224,... | collective-permute-start | bytes 98312 | tf_op jit(solution)/shard_map/ppermute | solution.py:27
Sparse Core Ops, SparseCore 0:
  204.9 74.5 all-gather.1
where the time goes:
time: 290 us; the launch traced here: 289 us
  local copies, waits for them, and re-layouts  96.7 us (33%)
  waiting for transfers between devices  83.5 us (29%)
  matrix products  43.2 us (15%)
  other arithmetic  33.4 us (12%)
  starting transfers between devices  16.2 us (6%)
  between operations  15.6 us (5%)
    mul x4, local copies, waits for them, and re-layouts, expand_cells(): shaped * occ.astype(jnp.float32)[:, None, :, None, :, None]  78.5 us
    all_gather x1, waiting for transfers between devices, local(): return lax.all_gather(pixels, 'cols', axis=1, tiled=True)  74.7 us
    dot_general x1, matrix products, local(): jnp.dot(in_front, optical.reshape(planes, columns * rows), precision=lax....  43.2 us
    reduce_sum x1, other arithmetic, local(): channels.append(jnp.sum(optical, axis=0))  17.9 us
    mul x1, other arithmetic, expand_cells(): shaped * occ.astype(jnp.float32)[:, None, :, None, :, None]  9.76 us
    mul x1, local copies, waits for them, and re-layouts, local(): 3.0 / (planes * slabs)  8.99 us
    unnamed x12, local copies, waits for them, and re-layouts  7.21 us
    ppermute x3, starting transfers between devices, from_partner(): return lax.ppermute(block, axis, route)  7.13 us
  transfers between devices with their start and end apart: 8, of which 5 were waited for; matrix products, arithmetic and copies ran while one was open for 28% of the time, Pallas kernels for 0%

commit v1 on v0

v1 whole, which is shorter than its diff:
```python
import functools

import jax
import jax.numpy as jnp
import numpy as np
from jax import lax
from jax.experimental import pallas as pl
from jax.experimental.pallas import tpu as pltpu
from jax.sharding import PartitionSpec as P

BX = 16
LOG2E = 1.4426950408889634


def shift_matrix(n):
    m = np.zeros((n, n), np.float32)
    for j in range(n):
        if j + 1 < n:
            m[j + 1, j] = 1.0
        if j >= 1:
            m[j - 1, j] = -1.0
    return jnp.asarray(m, jnp.bfloat16)


def render_kernel(light, pal, here, left, right, zlow, zhigh, xlow, xhigh, occ, diff,
                  out, field, rows_grad, image, edge):
    step = pl.program_id(0)
    last = pl.num_programs(0) - 1
    planes, _, rows = here.shape
    f32 = jnp.float32

    field[pl.ds(1, planes), 8:8 + BX, :] = here[...].astype(f32)
    field[pl.ds(1, planes), 0:8, :] = left[:, 8:16, :].astype(f32)
    field[pl.ds(1, planes), 8 + BX:16 + BX, :] = right[:, 0:8, :].astype(f32)
    field[0, 8:8 + BX, :] = zlow[...].astype(f32)
    field[planes + 1, 8:8 + BX, :] = zhigh[...].astype(f32)

    @pl.when(step == 0)
    def _():
        edge[...] = xlow[...].astype(f32)

        @pl.loop(0, planes)
        def _(z):
            field[z + 1, 0:8, :] = jnp.broadcast_to(edge[pl.ds(z, 1), :], (8, rows))

    @pl.when(step == last)
    def _():
        edge[...] = xhigh[...].astype(f32)

        @pl.loop(0, planes)
        def _(z):
            field[z + 1, 8 + BX:16 + BX, :] = jnp.broadcast_to(edge[pl.ds(z, 1), :], (8, rows))

    rows_grad[...] = jnp.dot(
        here[...].reshape(planes * BX, rows), diff[...], preferred_element_type=f32
    ).reshape(planes, BX, rows)

    l0, l1, l2 = light[0], light[1], light[2]
    half = [(0.5 * pal[c, 0], 0.5 * pal[c, 1]) for c in range(3)]
    ext0, ext1 = pal[3, 0] * LOG2E, pal[3, 1] * LOG2E
    group = 16

    def body(k, carry):
        total, through, red, green, blue, white = carry
        zb = planes // group - 1 - k
        scale = jnp.broadcast_to(occ[zb, pl.ds(step, 1), :], (BX, rows))
        base = zb * group
        for zi in range(group - 1, -1, -1):
            z = base + zi
            v = field[z + 1, 8:8 + BX, :]
            gz = field[z + 2, 8:8 + BX, :] - field[z, 8:8 + BX, :]
            gx = field[z + 1, 9:9 + BX, :] - field[z + 1, 7:7 + BX, :]
            gy = rows_grad[z]
            norm = lax.rsqrt((gz * gz + gx * gx) + (gy * gy + 4.0))
            facing = jnp.abs((gz * l0 + gx * l1 + gy * l2) * norm)
            shade = 0.3 + 0.7 * jnp.tanh(facing)
            total = total + scale * jnp.log2(1.0 + jnp.exp2(v * ext0 + ext1))
            beyond = jnp.exp2(total)
            weight = (through - beyond) * shade
            through = beyond
            red = red + weight * jnp.tanh(v * half[0][0] + half[0][1])
            green = green + weight * jnp.tanh(v * half[1][0] + half[1][1])
            blue = blue + weight * jnp.tanh(v * half[2][0] + half[2][1])
            white = white + weight
        return total, through, red, green, blue, white

    zero = jnp.zeros((BX, rows), f32)
    total, _, red, green, blue, white = lax.fori_loop(
        0, planes // group, body, (zero, zero + 1.0, zero, zero, zero, zero)
    )
    at = pl.ds(pl.multiple_of(step * BX, BX), BX)
    image[0, at, :] = 0.5 * (white + red)
    image[1, at, :] = 0.5 * (white + green)
    image[2, at, :] = 0.5 * (white + blue)
    image[3, at, :] = total

    @pl.when(step == last)
    def _():
        slabs, _, block, _ = out.shape
        for c in range(4):
            turned = image[c].T
            for d in range(slabs):
                out[d, c] = turned[d * block:(d + 1) * block, :]


def render(density, occupancy, light_dir, palette, zlow, zhigh, xlow, xhigh, slabs):
    planes, columns, rows = density.shape
    steps = columns // BX
    full = lambda *shape: pl.BlockSpec(shape, lambda i: (0,) * len(shape))
    block = lambda move: pl.BlockSpec((planes, BX, rows), lambda i: (0, move(i), 0))
    return pl.pallas_call(
        render_kernel,
        grid=(steps,),
        in_specs=[
            pl.BlockSpec(memory_space=pltpu.SMEM),
            pl.BlockSpec(memory_space=pltpu.SMEM),
            block(lambda i: i),
            block(lambda i: jnp.maximum(i - 1, 0)),
            block(lambda i: jnp.minimum(i + 1, steps - 1)),
            pl.BlockSpec((BX, rows), lambda i: (i, 0)),
            pl.BlockSpec((BX, rows), lambda i: (i, 0)),
            full(planes, rows),
            full(planes, rows),
            full(*occupancy.shape),
            full(rows, rows),
        ],
        out_specs=full(slabs, 4, rows // slabs, columns),
        out_shape=jax.ShapeDtypeStruct((slabs, 4, rows // slabs, columns), jnp.float32),
        scratch_shapes=[
            pltpu.VMEM((planes + 2, BX + 16, rows), jnp.float32),
            pltpu.VMEM((planes, BX, rows), jnp.float32),
            pltpu.VMEM((4, columns, rows), jnp.float32),
            pltpu.VMEM((planes, rows), jnp.float32),
        ],
        compiler_params=pltpu.CompilerParams(vmem_limit_bytes=48 * 1024 * 1024),
    )(light_dir, palette, density, density, density, zlow, zhigh, xlow, xhigh, occupancy,
      shift_matrix(rows))


def composite_kernel(parts, out):
    slabs = parts.shape[0]
    total = parts[slabs - 1, 3]
    colours = [parts[slabs - 1, c] for c in range(3)]
    for d in range(slabs - 2, -1, -1):
        through = jnp.exp2(total)
        colours = [colours[c] + through * parts[d, c] for c in range(3)]
        total = total + parts[d, 3]
    for c in range(3):
        out[c] = colours[c]
    out[3] = 1.0 - jnp.exp2(total)


def composite(parts):
    return pl.pallas_call(
        composite_kernel,
        out_shape=jax.ShapeDtypeStruct(parts.shape[1:], jnp.float32),
    )(parts)


def neighbours(axis, low, high):
    size = lax.axis_size(axis)
    up = [(i, i + 1) for i in range(size - 1)]
    down = [(j, i) for i, j in up]
    return lax.ppermute(high, axis, up), lax.ppermute(low, axis, down)


def local(density, occupancy, light_dir, palette):
    planes, columns, rows = density.shape
    slabs = lax.axis_size("depth")
    devices = lax.axis_size("cols")
    zlow, zhigh = neighbours("depth", density[0], density[-1])
    xlow, xhigh = neighbours("cols", density[:, 0, :], density[:, -1, :])
    scale = -3.0 / (planes * slabs)
    occ = jnp.repeat(occupancy.astype(jnp.float32) * scale, rows // occupancy.shape[2], axis=2)
    parts = render(density, occ, light_dir, palette, zlow, zhigh, xlow, xhigh, slabs)
    parts = lax.all_to_all(parts, "depth", 0, 0, tiled=True)
    pixels = composite(parts)
    spread = jnp.broadcast_to(pixels[None], (devices,) + pixels.shape)
    image = lax.all_to_all(spread, "cols", 0, 0, tiled=True)
    return image.transpose(1, 0, 3, 2).reshape(4, devices * columns, rows // slabs)


def solution(mesh):
    placed = (P("depth", "cols", None), P("depth", "cols", None), P(), P())
    return jax.shard_map(
        local, mesh=mesh, in_specs=placed, out_specs=P(None, None, "depth"), check_vma=False
    )
```

time: 290 us -> 97.9 us (0.34)
  local copies, waits for them, and re-layouts: 96.7 us -> 8.57 us
  waiting for transfers between devices: 83.5 us -> 1.77 us
  blocking collectives: 0 us -> 52.9 us
  matrix products: 43.2 us -> 0 us
  other arithmetic: 33.4 us -> 0.72 us
  Pallas kernels: 0 us -> 23 us
  between operations: 15.6 us -> 0.11 us
  starting transfers between devices: 16.2 us -> 10.2 us
    mul x5 -> x1, local copies, waits for them, and re-layouts: 87.5 us -> 0.12 us  [local(): occupancy.astype(jnp.float32) * scale]
    all_gather x1 -> x0, waiting for transfers between devices: 74.7 us -> none  [local(): return lax.all_gather(pixels, 'cols', axis=1, tiled=True)]
    all_to_all x0 -> x2, blocking collectives: none -> 52.9 us  [the longest x1 41.2 us: local(): image = lax.all_to_all(spread, 'cols', 0, 0, tiled=True)]
    dot_general x1 -> x0, matrix products: 43.2 us -> none  [local(): jnp.dot(in_front, optical.reshape(planes, columns * rows), precision=lax....]
    pallas_call x0 -> x2, Pallas kernels: none -> 23 us  [the longest x1 21.4 us: render(): pl.pallas_call(render_kernel, grid=(steps,), in_specs=[pl.BlockSpec(memor...]
    reduce_sum x1 -> x0, other arithmetic: 17.9 us -> none  [local(): channels.append(jnp.sum(optical, axis=0))]
    mul x4 -> x1, other arithmetic: 9.79 us -> 0.72 us  [local(): occupancy.astype(jnp.float32) * scale]
    ppermute x7 -> x4, waiting for transfers between devices: 8.79 us -> 1.77 us  [neighbours(): return (lax.ppermute(high, axis, up), lax.ppermute(low, axis, down))]
  transfers between devices with their start and end apart: 8 -> 4, of which waited for: 5 -> 1; matrix products, arithmetic and copies ran while one was open for 28% -> 3% of each run, Pallas kernels for 0% -> 0%
where the time goes in v1:
time: 97.9 us; the launch traced here: 97.3 us
  blocking collectives  52.9 us (54%)
  Pallas kernels  23 us (23%)
  starting transfers between devices  10.2 us (10%)
  local copies, waits for them, and re-layouts  8.57 us (9%)
  waiting for transfers between devices  1.77 us (2%)
    all_to_all x1, blocking collectives, local(): image = lax.all_to_all(spread, 'cols', 0, 0, tiled=True)  41.2 us
    pallas_call x1, Pallas kernels, render(): pl.pallas_call(render_kernel, grid=(steps,), in_specs=[pl.BlockSpec(memor...  21.4 us
    all_to_all x1, blocking collectives, local(): parts = lax.all_to_all(parts, 'depth', 0, 0, tiled=True)  11.8 us
    ppermute x4, starting transfers between devices, neighbours(): return (lax.ppermute(high, axis, up), lax.ppermute(low, axis, down))  10.2 us
    unnamed x9, local copies, waits for them, and re-layouts  4.38 us
  transfers between devices with their start and end apart: 4, of which 1 were waited for; matrix products, arithmetic and copies ran while one was open for 3% of the time, Pallas kernels for 0%

profile of v1, /device:TPU:2, one launch (start us, length us, event | category | flops | bytes accessed | tf_op | source)
XLA Modules:
  0.0 97.3 jit_solution(14927961372507288933)
XLA Ops:
  0.0 0.8 slice_bitcast_fusion
  0.8 1.3 %collective-permute-start.1 = (bf16[128,128]{1,0:T(8,128)(2,1)S(1)}, bf16[128,128]{1,0:T(8,128)(2,1)S(1)}, u32[]{:S(2)}, u32[]{:S(2)}) collective-permute-start(bf16[128,128]{1,0:T(8,128)(2,1)S(1)} %get-tuple-element.7), channel_id=1, source_target_pairs={{32,0},{64,32},{96,64},{128,96},{160,128},{192,160},{224,192},{33,... | collective-permute-start | bytes 98312 | tf_op jit(solution)/shard_map/ppermute | solution.py:164
  2.1 3.0 %collective-permute-start = (bf16[128,128]{1,0:T(8,128)(2,1)S(1)}, bf16[128,128]{1,0:T(8,128)(2,1)S(1)}, u32[]{:S(2)}, u32[]{:S(2)}) collective-permute-start(bf16[128,128]{1,0:T(8,128)(2,1)S(1)} %get-tuple-element.8), channel_id=1, source_target_pairs={{0,32},{32,64},{64,96},{96,128},{128,160},{160,192},{192,224},{1,3... | collective-permute-start | bytes 98312 | tf_op jit(solution)/shard_map/ppermute | solution.py:164
  5.1 1.1 %fusion = (bf16[128,1,128]{2,1,0:T(2,128)(2,1)S(1)}, bf16[128,1,128]{2,1,0:T(2,128)(2,1)S(1)}) fusion(bf16[128,128,128]{2,1,0:T(8,128)(2,1)} %right.1), kind=kLoop, calls=%fused_computation.6 | loop fusion | bytes 131072 | tf_op jit(solution)/shard_map/slice | solution.py:172
  6.3 3.4 %collective-permute-start.2 = (bf16[128,128]{1,0:T(8,128)(2,1)S(1)}, bf16[128,128]{1,0:T(8,128)(2,1)S(1)}, u32[]{:S(2)}, u32[]{:S(2)}) collective-permute-start(bf16[128,128]{1,0:T(8,128)(2,1)S(1)} %bitcast.16), channel_id=1, source_target_pairs={{0,1},{1,2},{2,3},{3,4},{4,5},{5,6},{6,7},{7,8},{8,9},{9,10},{10,1... | collective-permute-start | bytes 98312 | tf_op jit(solution)/shard_map/ppermute | solution.py:164
  9.7 2.4 %collective-permute-start.3 = (bf16[128,128]{1,0:T(8,128)(2,1)S(1)}, bf16[128,128]{1,0:T(8,128)(2,1)S(1)}, u32[]{:S(2)}, u32[]{:S(2)}) collective-permute-start(bf16[128,128]{1,0:T(8,128)(2,1)S(1)} %bitcast.17), channel_id=1, source_target_pairs={{1,0},{2,1},{3,2},{4,3},{5,4},{6,5},{7,6},{8,7},{9,8},{10,9},{11,1... | collective-permute-start | bytes 98312 | tf_op jit(solution)/shard_map/ppermute | solution.py:164
  12.1 0.7 convert_multiply_fusion
  12.9 0.8 copy.17.pal
  13.6 0.1 copy.16
  13.8 0.1 broadcast_in_dim.4
  13.9 0.1 reshape.7.occ
  14.0 0.0 collective-permute-done.1.zhigh
  14.0 0.0 collective-permute-done.zlow
  14.0 0.0 collective-permute-done.2.xlow
  14.0 1.8 %collective-permute-done.3.xhigh = bf16[128,128]{1,0:T(8,128)(2,1)S(1)} collective-permute-done((bf16[128,128]{1,0:T(8,128)(2,1)S(1)}, bf16[128,128]{1,0:T(8,128)(2,1)S(1)}, u32[]{:S(2)}, u32[]{:S(2)}) %collective-permute-start.3) | collective-permute-done | bytes 32800 | tf_op jit(solution)/shard_map/ppermute | solution.py:164
  15.8 0.0 copy-start
  15.8 2.2 %copy-done = bf16[128,128,128]{2,1,0:T(8,128)(2,1)S(1)} copy-done((bf16[128,128,128]{2,1,0:T(8,128)(2,1)S(1)}, bf16[128,128,128]{2,1,0:T(8,128)(2,1)}, u32[]{:S(2)}) %copy-start) | copy-done | bytes 4194328
  18.0 0.0 copy-start.1
  18.0 0.8 copy-done.1
  18.7 0.0 copy-start.2
  18.7 0.7 copy-done.2
  19.4 21.4 %shard_map.55 = f32[8,4,16,128]{3,2,1,0:T(8,128)S(1)} custom-call(f32[3]{0:T(128)S(1)} %copy-done.2, f32[4,2]{1,0:T(4,128)S(1)} %copy.17.pal, bf16[128,128,128]{2,1,0:T(8,128)(2,1)S(1)} %copy-done, bf16[128,128,128]{2,1,0:T(8,128)(2,1)S(1)} %copy-done, bf16[128,128,128]{2,1,0:T(8,128)(2,1)S(1)} %copy-done, bf16[128,128]{1,0:T(8,128)(2,1)S(1)} %collective-permute-done.zlow, ...), custom_call_target="tpu_custom_call" | custom-call | tf_op jit(solution)/shard_map/pallas_call | solution.py:111
  40.8 11.8 %all_to_all.10.parts = f32[8,4,16,128]{3,2,1,0:T(8,128)} all-to-all(f32[8,4,16,128]{3,2,1,0:T(8,128)S(1)} %shard_map.55), channel_id=1, replica_groups=mesh['depth'=8,'cols'=32] {'depth'}, dimensions={0} | all-to-all | bytes 524288 | tf_op jit(solution)/shard_map/all_to_all | solution.py:176
  52.6 1.6 %shard_map.56 = f32[4,16,128]{2,1,0:T(8,128)} custom-call(f32[8,4,16,128]{3,2,1,0:T(8,128)} %all_to_all.10.parts), custom_call_target="tpu_custom_call" | custom-call | tf_op jit(solution)/shard_map/pallas_call | solution.py:154
  54.2 0.9 broadcast_in_dim.10
  55.1 41.2 %all_to_all.11 = f32[32,4,16,128]{3,2,1,0:T(8,128)S(1)} all-to-all(f32[32,4,16,128]{3,2,1,0:T(8,128)S(1)} %broadcast_in_dim.10), channel_id=1, replica_groups=mesh['depth'=8,'cols'=32] {'cols'}, dimensions={0} | all-to-all | bytes 2097152 | tf_op jit(solution)/shard_map/all_to_all | solution.py:179
  96.2 1.0 %copy_bitcast_fusion = f32[4,4096,16]{1,2,0:T(8,128)} fusion(f32[32,4,16,128]{3,2,1,0:T(8,128)S(1)} %all_to_all.11), kind=kLoop, calls=%fused_computation | loop fusion | bytes 2097152 | tf_op jit(solution)/shard_map/reshape | solution.py:180
  (2 shorter events, 0.0 us)
Async XLA Ops:
  0.8 13.2 %collective-permute-start.1 = (bf16[128,128]{1,0:T(8,128)(2,1)S(1)}, bf16[128,128]{1,0:T(8,128)(2,1)S(1)}, u32[]{:S(2)}, u32[]{:S(2)}) collective-permute-start(bf16[128,128]{1,0:T(8,128)(2,1)S(1)} %get-tuple-element.7), channel_id=1, source_target_pairs={{32,0},{64,32},{96,64},{128,96},{160,128},{192,160},{224,192},{33,... | collective-permute-start | bytes 98312 | tf_op jit(solution)/shard_map/ppermute | solution.py:164
  2.1 12.0 %collective-permute-start = (bf16[128,128]{1,0:T(8,128)(2,1)S(1)}, bf16[128,128]{1,0:T(8,128)(2,1)S(1)}, u32[]{:S(2)}, u32[]{:S(2)}) collective-permute-start(bf16[128,128]{1,0:T(8,128)(2,1)S(1)} %get-tuple-element.8), channel_id=1, source_target_pairs={{0,32},{32,64},{64,96},{96,128},{128,160},{160,192},{192,224},{1,3... | collective-permute-start | bytes 98312 | tf_op jit(solution)/shard_map/ppermute | solution.py:164
  6.3 7.8 %collective-permute-start.2 = (bf16[128,128]{1,0:T(8,128)(2,1)S(1)}, bf16[128,128]{1,0:T(8,128)(2,1)S(1)}, u32[]{:S(2)}, u32[]{:S(2)}) collective-permute-start(bf16[128,128]{1,0:T(8,128)(2,1)S(1)} %bitcast.16), channel_id=1, source_target_pairs={{0,1},{1,2},{2,3},{3,4},{4,5},{5,6},{6,7},{7,8},{8,9},{9,10},{10,1... | collective-permute-start | bytes 98312 | tf_op jit(solution)/shard_map/ppermute | solution.py:164
  9.7 6.1 %collective-permute-start.3 = (bf16[128,128]{1,0:T(8,128)(2,1)S(1)}, bf16[128,128]{1,0:T(8,128)(2,1)S(1)}, u32[]{:S(2)}, u32[]{:S(2)}) collective-permute-start(bf16[128,128]{1,0:T(8,128)(2,1)S(1)} %bitcast.17), channel_id=1, source_target_pairs={{1,0},{2,1},{3,2},{4,3},{5,4},{6,5},{7,6},{8,7},{9,8},{10,9},{11,1... | collective-permute-start | bytes 98312 | tf_op jit(solution)/shard_map/ppermute | solution.py:164
  15.8 2.2 %copy-start = (bf16[128,128,128]{2,1,0:T(8,128)(2,1)S(1)}, bf16[128,128,128]{2,1,0:T(8,128)(2,1)}, u32[]{:S(2)}) copy-start(bf16[128,128,128]{2,1,0:T(8,128)(2,1)} %right.1) | copy-start | bytes 12582916
  18.0 0.8 copy-start.1
  18.7 0.7 copy-start.2

commit v2 on v1

v2 whole, which is shorter than its diff:
```python
import jax
import jax.numpy as jnp
from jax import lax
from jax.experimental import pallas as pl
from jax.experimental.pallas import tpu as pltpu
from jax.sharding import PartitionSpec as P

BX = 16
LOG2E = 1.4426950408889634
CODE_TOP = 65535.0
CODE_STEP = CODE_TOP / 24.0
INNER_LIMIT = 20 * 1024 * 1024
OUTER_LIMIT = 16 * 1024 * 1024


def difference_matrix(rows):
    row = lax.broadcasted_iota(jnp.int32, (rows, rows), 0)
    col = lax.broadcasted_iota(jnp.int32, (rows, rows), 1)
    ahead = (row == col + 1).astype(jnp.float32)
    behind = (row + 1 == col).astype(jnp.float32)
    return (ahead - behind).astype(jnp.bfloat16)


def occupied_row(occ, zb, xb, rows, scale):
    parts = occ.shape[1]
    lane = lax.broadcasted_iota(jnp.int32, (BX, rows), 1)
    value = jnp.broadcast_to(occ[zb, parts - 1, xb], (BX, rows))
    for part in range(parts - 2, -1, -1):
        value = jnp.where(lane < (part + 1) * (rows // parts), occ[zb, part, xb], value)
    return value.astype(jnp.float32) * scale


def shade_terms(v, gz, gx, gy, light):
    norm = lax.rsqrt((gz * gz + gx * gx) + (gy * gy + 4.0))
    facing = (gz * light[0] + gx * light[1]) + gy * light[2]
    return jnp.abs(jnp.tanh(facing * norm)) + 3.0 / 7.0


def optical_term(v, coeff):
    return jnp.log2(1.0 + jnp.exp2(v * coeff[3][0] + coeff[3][1]))


def coefficients(pal):
    coeff = [(0.5 * pal[0, c], 0.5 * pal[1, c]) for c in range(3)]
    return coeff + [(pal[0, 3] * LOG2E, pal[1, 3] * LOG2E)]


def march(field, at, gradient, scale_of, light, coeff, planes, group, rows, ends):
    f32 = jnp.float32
    lights = [light[i] for i in range(3)]

    def body(k, carry):
        total, through, red, green, blue, white = carry
        zb = planes // group - 1 - k
        scale = scale_of(zb)
        base = zb * group
        gys = gradient(base)
        for zi in range(group - 1, -1, -1):
            z = base + zi
            v = field[z + 1, pl.ds(at + 1, BX), :]
            gz = field[z + 2, pl.ds(at + 1, BX), :] - field[z, pl.ds(at + 1, BX), :]
            gx = field[z + 1, pl.ds(at + 2, BX), :] - field[z + 1, pl.ds(at, BX), :]
            gy = gys[zi * BX:(zi + 1) * BX]
            total = total + scale * optical_term(v, coeff)
            beyond = jnp.exp2(total)
            weight = (through - beyond) * shade_terms(v, gz, gx, gy, lights)
            if not ends and zi == 0:
                weight = weight * (zb > 0).astype(f32)
            if not ends and zi == group - 1:
                weight = weight * (k > 0).astype(f32)
            through = beyond
            red = red + weight * jnp.tanh(v * coeff[0][0] + coeff[0][1])
            green = green + weight * jnp.tanh(v * coeff[1][0] + coeff[1][1])
            blue = blue + weight * jnp.tanh(v * coeff[2][0] + coeff[2][1])
            white = white + weight
        return total, through, red, green, blue, white

    zero = jnp.zeros((BX, rows), f32)
    total, _, red, green, blue, white = lax.fori_loop(
        0, planes // group, body, (zero, zero + 1.0, zero, zero, zero, zero)
    )
    return [0.35 * (white + red), 0.35 * (white + green), 0.35 * (white + blue), total]


def inner_kernel(scale, light, pal, occ, density, image, field, diff):
    planes, columns, rows = density.shape
    group = planes // occ.shape[0]
    diff[...] = difference_matrix(rows)
    field[0] = jnp.zeros((columns, rows), jnp.float32)
    field[planes + 1] = jnp.zeros((columns, rows), jnp.float32)

    @pl.loop(0, planes // 4)
    def _(k):
        for j in range(4):
            field[4 * k + j + 1] = density[4 * k + j].astype(jnp.float32)

    coeff = coefficients(pal)

    @pl.loop(1, columns // BX - 1)
    def _(block):
        first = pl.multiple_of(block * BX, BX)

        def gradient(base):
            piece = density[pl.ds(base, group), pl.ds(first, BX), :].reshape(group * BX, rows)
            return jnp.dot(piece, diff[...], preferred_element_type=jnp.float32)

        sums = march(
            field, first - 1, gradient, lambda zb: occupied_row(occ, zb, block, rows, scale),
            light, coeff, planes, group, rows, False,
        )
        for c in range(4):
            image[c, pl.ds(first, BX), :] = sums[c]


def outer_kernel(scale, light, pal, occ, density, image, zlow, zhigh, xlow, xhigh, out,
                 field, edge, whole):
    planes, columns, rows = density.shape
    group = planes // occ.shape[0]
    f32 = jnp.float32
    diff = difference_matrix(rows)
    coeff = coefficients(pal)
    last = columns // BX - 1
    lights = [light[i] for i in range(3)]
    whole[...] = image[...]

    for block, halo in ((0, xlow), (last, xhigh)):
        first = block * BX
        field[pl.ds(1, planes), 8:8 + BX, :] = density[:, first:first + BX, :].astype(f32)
        field[0, 8:8 + BX, :] = zlow[first:first + BX, :].astype(f32)
        field[planes + 1, 8:8 + BX, :] = zhigh[first:first + BX, :].astype(f32)
        edge[...] = halo[...].astype(f32)
        if block == 0:
            field[pl.ds(1, planes), 8 + BX:16 + BX, :] = density[:, BX:BX + 8, :].astype(f32)
            spot = 0
        else:
            field[pl.ds(1, planes), 0:8, :] = density[:, first - 8:first, :].astype(f32)
            spot = 8 + BX

        @pl.loop(0, planes // 8)
        def _(k):
            for j in range(8):
                row = edge[pl.ds(8 * k + j, 1), :]
                field[8 * k + j + 1, spot:spot + 8, :] = jnp.broadcast_to(row, (8, rows))

        def gradient(base):
            piece = density[pl.ds(base, group), first:first + BX, :].reshape(group * BX, rows)
            return jnp.dot(piece, diff, preferred_element_type=f32)

        sums = march(
            field, 7, gradient, lambda zb: occupied_row(occ, zb, block, rows, scale),
            light, coeff, planes, group, rows, True,
        )
        for c in range(4):
            whole[c, first:first + BX, :] = sums[c]

    for block in range(1, last):
        at = slice(block * BX, (block + 1) * BX)
        total = whole[3, at, :]
        for z in (planes - 1, 0):
            plane = density[z].astype(f32)
            v = plane[at]
            if z == 0:
                gz = density[1, at, :].astype(f32) - zlow[at, :].astype(f32)
            else:
                gz = zhigh[at, :].astype(f32) - density[z - 1, at, :].astype(f32)
            gx = plane[at.start + 1:at.stop + 1] - plane[at.start - 1:at.stop - 1]
            gy = jnp.dot(density[z, at, :], diff, preferred_element_type=f32)
            here = occupied_row(occ, z // group, block, rows, scale) * optical_term(v, coeff)
            if z == 0:
                weight = jnp.exp2(total - here) - jnp.exp2(total)
            else:
                weight = 1.0 - jnp.exp2(here)
            weight = weight * shade_terms(v, gz, gx, gy, lights) * 0.35
            for c in range(3):
                whole[c, at, :] += weight + weight * jnp.tanh(v * coeff[c][0] + coeff[c][1])

    slabs, _, share, _ = out.shape
    for c in range(4):
        turned = whole[c].T
        for d in range(slabs):
            out[d, c] = turned[d * share:(d + 1) * share, :]


def smem():
    return pl.BlockSpec(memory_space=pltpu.SMEM)


def vmem():
    return pl.BlockSpec(memory_space=pltpu.VMEM)


def render_inner(density, occ, light_dir, pal, scale):
    planes, columns, rows = density.shape
    return pl.pallas_call(
        lambda *refs: inner_kernel(scale, *refs),
        in_specs=[smem(), smem(), smem(), vmem()],
        out_specs=vmem(),
        out_shape=jax.ShapeDtypeStruct((4, columns, rows), jnp.float32),
        scratch_shapes=[
            pltpu.VMEM((planes + 2, columns, rows), jnp.float32),
            pltpu.VMEM((rows, rows), jnp.bfloat16),
        ],
        cost_estimate=pl.CostEstimate(
            flops=40 * density.size, bytes_accessed=2 * density.size,
            transcendentals=8 * density.size,
        ),
        compiler_params=pltpu.CompilerParams(vmem_limit_bytes=INNER_LIMIT),
    )(light_dir, pal, occ, density)


def render_outer(density, occ, light_dir, pal, image, halos, scale, slabs):
    planes, columns, rows = density.shape
    return pl.pallas_call(
        lambda *refs: outer_kernel(scale, *refs),
        in_specs=[smem(), smem(), smem()] + [vmem()] * 6,
        out_specs=vmem(),
        out_shape=jax.ShapeDtypeStruct((slabs, 4, rows // slabs, columns), jnp.float32),
        scratch_shapes=[
            pltpu.VMEM((planes + 2, BX + 16, rows), jnp.float32),
            pltpu.VMEM((planes, rows), jnp.float32),
            pltpu.VMEM((4, columns, rows), jnp.float32),
        ],
        compiler_params=pltpu.CompilerParams(vmem_limit_bytes=OUTER_LIMIT),
    )(light_dir, pal, occ, density, image, *halos)


def composite_kernel(parts, out):
    slabs = parts.shape[0]
    total = parts[slabs - 1, 3]
    colours = [parts[slabs - 1, c] for c in range(3)]
    for d in range(slabs - 2, -1, -1):
        through = jnp.exp2(total)
        colours = [colours[c] + through * parts[d, c] for c in range(3)]
        total = total + parts[d, 3]
    colours.append(1.0 - jnp.exp2(total))
    for c in range(4):
        level = jnp.log2(jnp.maximum(colours[c], 2.0 ** -24))
        code = (level * CODE_STEP + (CODE_TOP + 0.5)).astype(jnp.int32) - 32768
        code = code.astype(jnp.int16)
        for k in range(out.shape[0]):
            out[k, c] = code


def composite(parts, devices):
    return pl.pallas_call(
        composite_kernel,
        out_shape=jax.ShapeDtypeStruct((devices,) + parts.shape[1:], jnp.int16),
    )(parts)


def decode_kernel(codes, out):
    devices, _, share, columns = codes.shape
    for k in range(devices):
        code = codes[k, 0].astype(jnp.int32) + 32768
        value = jnp.exp2((code.astype(jnp.float32) - CODE_TOP) * (1.0 / CODE_STEP))
        out[0, :, k * columns:(k + 1) * columns] = jnp.where(code > 0, value, 0.0)


def decode(codes):
    devices, channels, share, columns = codes.shape
    return pl.pallas_call(
        decode_kernel,
        grid=(channels,),
        in_specs=[pl.BlockSpec((devices, 1, share, columns), lambda c: (0, c, 0, 0))],
        out_specs=pl.BlockSpec((1, share, devices * columns), lambda c: (c, 0, 0)),
        out_shape=jax.ShapeDtypeStruct((channels, share, devices * columns), jnp.float32),
    )(codes)


def neighbours(axis, low, high):
    size = lax.axis_size(axis)
    up = [(i, i + 1) for i in range(size - 1)]
    down = [(j, i) for i, j in up]
    return lax.ppermute(high, axis, up), lax.ppermute(low, axis, down)


def local(density, occupancy, light_dir, palette):
    planes, columns, rows = density.shape
    slabs = lax.axis_size("depth")
    devices = lax.axis_size("cols")
    scale = -3.0 / (planes * slabs)
    xhalo = neighbours("cols", density[:, 0, :], density[:, -1, :])
    zhalo = neighbours("depth", density[0], density[-1])
    occ = occupancy.transpose(0, 2, 1)
    pal = palette.T
    image = render_inner(density, occ, light_dir, pal, scale)
    parts = render_outer(density, occ, light_dir, pal, image, zhalo + xhalo, scale, slabs)
    parts = lax.all_to_all(parts, "depth", 0, 0, tiled=True)
    codes = composite(parts, devices)
    codes = lax.all_to_all(codes, "cols", 0, 0, tiled=True)
    return decode(codes).transpose(0, 2, 1)


def solution(mesh):
    placed = (P("depth", "cols", None), P("depth", "cols", None), P(), P())
    return jax.shard_map(
        local, mesh=mesh, in_specs=placed, out_specs=P(None, None, "depth"), check_vma=False
    )
```

time: 97.9 us -> 83.9 us (0.86)
  blocking collectives: 52.9 us -> 41.1 us
  Pallas kernels: 23 us -> 25.7 us
  local copies, waits for them, and re-layouts: 8.57 us -> 6.18 us
  waiting for transfers between devices: 1.77 us -> 0.01 us
    all_to_all x1, blocking collectives: 41.2 us -> 29 us  [local(): codes = lax.all_to_all(codes, 'cols', 0, 0, tiled=True)]
    pallas_call x2 -> x4, Pallas kernels: 23 us -> 25.7 us  [the longest x1 14.5 us: render_inner(): pl.pallas_call(lambda *refs: inner_kernel(scale, *refs), in_specs=[smem()...]
    ppermute x4, waiting for transfers between devices: 1.77 us -> 0.01 us  [neighbours(): return (lax.ppermute(high, axis, up), lax.ppermute(low, axis, down))]
    reshape x2 -> x0, local copies, waits for them, and re-layouts: 1.16 us -> none  [the longest x1 1.04 us: local(): image.transpose(1, 0, 3, 2).reshape(4, devices * columns, rows // slabs)]
    broadcast_in_dim x2 -> x0, local copies, waits for them, and re-layouts: 0.99 us -> none  [the longest x1 0.86 us: local(): spread = jnp.broadcast_to(pixels[None], (devices,) + pixels.shape)]
    unnamed x9 -> x12, local copies, waits for them, and re-layouts: 4.38 us -> 4.25 us
  transfers between devices with their start and end apart: 4 -> 4, of which waited for: 1 -> 0; matrix products, arithmetic and copies ran while one was open for 3% -> 1% of each run, Pallas kernels for 0% -> 17%
where the time goes in v2:
time: 83.9 us; the launch traced here: 83.3 us
  blocking collectives  41.1 us (49%)
  Pallas kernels  25.7 us (31%)
  starting transfers between devices  10.2 us (12%)
  local copies, waits for them, and re-layouts  6.18 us (7%)
    all_to_all x1, blocking collectives, local(): codes = lax.all_to_all(codes, 'cols', 0, 0, tiled=True)  29 us
    pallas_call x1, Pallas kernels, render_inner(): pl.pallas_call(lambda *refs: inner_kernel(scale, *refs), in_specs=[smem()...  14.5 us
    all_to_all x1, blocking collectives, local(): parts = lax.all_to_all(parts, 'depth', 0, 0, tiled=True)  12 us
    ppermute x4, starting transfers between devices, neighbours(): return (lax.ppermute(high, axis, up), lax.ppermute(low, axis, down))  10.2 us
    pallas_call x1, Pallas kernels, render_outer(): pl.pallas_call(lambda *refs: outer_kernel(scale, *refs), in_specs=[smem()...  5.96 us
    unnamed x12, local copies, waits for them, and re-layouts  4.25 us
    pallas_call x1, Pallas kernels, decode(): pl.pallas_call(decode_kernel, grid=(channels,), in_specs=[pl.BlockSpec((d...  3.38 us
    pallas_call x1, Pallas kernels, composite(): pl.pallas_call(composite_kernel, out_shape=jax.ShapeDtypeStruct((devices,...  1.89 us
  transfers between devices with their start and end apart: 4, of which 0 were waited for; matrix products, arithmetic and copies ran while one was open for 1% of the time, Pallas kernels for 17%

profile of v2, /device:TPU:2, one launch (start us, length us, event | category | flops | bytes accessed | tf_op | source)
XLA Modules:
  0.0 83.3 jit_solution(13697056024705518533)
XLA Ops:
  0.0 0.8 slice_bitcast_fusion
  0.8 1.3 %collective-permute-start.1 = (bf16[128,128]{1,0:T(8,128)(2,1)S(1)}, bf16[128,128]{1,0:T(8,128)(2,1)S(1)}, u32[]{:S(2)}, u32[]{:S(2)}) collective-permute-start(bf16[128,128]{1,0:T(8,128)(2,1)S(1)} %get-tuple-element.7), channel_id=1, source_target_pairs={{32,0},{64,32},{96,64},{128,96},{160,128},{192,160},{224,192},{33,... | collective-permute-start | bytes 98312 | tf_op jit(solution)/shard_map/ppermute | solution.py:274
  2.1 3.0 %collective-permute-start = (bf16[128,128]{1,0:T(8,128)(2,1)S(1)}, bf16[128,128]{1,0:T(8,128)(2,1)S(1)}, u32[]{:S(2)}, u32[]{:S(2)}) collective-permute-start(bf16[128,128]{1,0:T(8,128)(2,1)S(1)} %get-tuple-element.8), channel_id=1, source_target_pairs={{0,32},{32,64},{64,96},{96,128},{128,160},{160,192},{192,224},{1,3... | collective-permute-start | bytes 98312 | tf_op jit(solution)/shard_map/ppermute | solution.py:274
  5.1 1.1 %fusion = (bf16[128,1,128]{2,1,0:T(2,128)(2,1)S(1)}, bf16[128,1,128]{2,1,0:T(2,128)(2,1)S(1)}) fusion(bf16[128,128,128]{2,1,0:T(8,128)(2,1)} %refs_3_.3), kind=kLoop, calls=%fused_computation.4 | loop fusion | bytes 131072 | tf_op jit(solution)/shard_map/slice | solution.py:282
  6.3 3.4 %collective-permute-start.2 = (bf16[128,128]{1,0:T(8,128)(2,1)S(1)}, bf16[128,128]{1,0:T(8,128)(2,1)S(1)}, u32[]{:S(2)}, u32[]{:S(2)}) collective-permute-start(bf16[128,128]{1,0:T(8,128)(2,1)S(1)} %bitcast.17), channel_id=1, source_target_pairs={{0,1},{1,2},{2,3},{3,4},{4,5},{5,6},{6,7},{7,8},{8,9},{9,10},{10,1... | collective-permute-start | bytes 98312 | tf_op jit(solution)/shard_map/ppermute | solution.py:274
  9.7 2.4 %collective-permute-start.3 = (bf16[128,128]{1,0:T(8,128)(2,1)S(1)}, bf16[128,128]{1,0:T(8,128)(2,1)S(1)}, u32[]{:S(2)}, u32[]{:S(2)}) collective-permute-start(bf16[128,128]{1,0:T(8,128)(2,1)S(1)} %bitcast.18), channel_id=1, source_target_pairs={{1,0},{2,1},{3,2},{4,3},{5,4},{6,5},{7,6},{8,7},{9,8},{10,9},{11,1... | collective-permute-start | bytes 98312 | tf_op jit(solution)/shard_map/ppermute | solution.py:274
  12.1 0.0 copy-start
  12.2 2.2 %copy-done = bf16[128,128,128]{2,1,0:T(8,128)(2,1)S(1)} copy-done((bf16[128,128,128]{2,1,0:T(8,128)(2,1)S(1)}, bf16[128,128,128]{2,1,0:T(8,128)(2,1)}, u32[]{:S(2)}) %copy-start) | copy-done | bytes 4194328
  14.3 0.0 copy-start.2
  14.3 0.7 copy-done.2
  15.1 0.0 copy-start.3
  15.1 0.7 copy-done.3
  15.7 0.0 copy-start.4
  15.7 0.7 copy-done.4
  16.4 0.0 copy-start.1
  16.4 14.5 %shard_map.46.refs_4_ = f32[4,128,128]{2,1,0:T(8,128)S(1)} custom-call(f32[3]{0:T(128)S(1)} %copy-done.4, f32[2,4]{1,0:T(2,128)S(1)} %bitcast.15, s32[8,4,8]{2,1,0:T(4,128)S(1)} %bitcast.13, bf16[128,128,128]{2,1,0:T(8,128)(2,1)S(1)} %copy-done), custom_call_target="tpu_custom_call" | custom-call | flops 83886080 | bytes 4194304 | tf_op jit(solution)/shard_map/pallas_call | solution.py:194
  30.9 0.0 collective-permute-done.1.refs_6_
  30.9 0.0 collective-permute-done.refs_5_
  30.9 0.0 collective-permute-done.2.refs_7_
  30.9 0.0 collective-permute-done.3.refs_8_
  30.9 0.0 copy-done.1
  30.9 6.0 %shard_map.47 = f32[8,4,16,128]{3,2,1,0:T(8,128)S(1)} custom-call(f32[3]{0:T(128)S(1)} %copy-done.4, f32[2,4]{1,0:T(2,128)S(1)} %bitcast.16, s32[8,4,8]{2,1,0:T(4,128)S(1)} %bitcast.14, bf16[128,128,128]{2,1,0:T(8,128)(2,1)S(1)} %copy-done.1, f32[4,128,128]{2,1,0:T(8,128)S(1)} %shard_map.46.refs_4_, bf16[128,128]{1,0:T(8,128)(2,1)S(1)} %collective-permute-done.refs_5_, ...), custom_call_target="tpu_custom_call" | custom-call | tf_op jit(solution)/shard_map/pallas_call | solution.py:213
  36.9 12.0 %all_to_all.10.parts = f32[8,4,16,128]{3,2,1,0:T(8,128)} all-to-all(f32[8,4,16,128]{3,2,1,0:T(8,128)S(1)} %shard_map.47), channel_id=1, replica_groups=mesh['depth'=8,'cols'=32] {'depth'}, dimensions={0} | all-to-all | bytes 524288 | tf_op jit(solution)/shard_map/all_to_all | solution.py:288
  48.9 1.9 %shard_map.48 = s16[32,4,16,128]{3,2,1,0:T(8,128)(2,1)} custom-call(f32[8,4,16,128]{3,2,1,0:T(8,128)} %all_to_all.10.parts), custom_call_target="tpu_custom_call" | custom-call | tf_op jit(solution)/shard_map/pallas_call | solution.py:245
  50.8 29.0 %all_to_all.11.codes = s16[32,4,16,128]{3,2,1,0:T(8,128)(2,1)} all-to-all(s16[32,4,16,128]{3,2,1,0:T(8,128)(2,1)} %shard_map.48), channel_id=1, replica_groups=mesh['depth'=8,'cols'=32] {'cols'}, dimensions={0} | all-to-all | bytes 1048576 | tf_op jit(solution)/shard_map/all_to_all | solution.py:290
  79.9 3.4 %shard_map.49 = f32[4,16,4096]{2,1,0:T(8,128)} custom-call(s16[32,4,16,128]{3,2,1,0:T(8,128)(2,1)} %all_to_all.11.codes), custom_call_target="tpu_custom_call" | custom-call | tf_op jit(solution)/shard_map/pallas_call | solution.py:261
  (2 shorter events, 0.0 us)
Async XLA Ops:
  0.8 30.1 %collective-permute-start.1 = (bf16[128,128]{1,0:T(8,128)(2,1)S(1)}, bf16[128,128]{1,0:T(8,128)(2,1)S(1)}, u32[]{:S(2)}, u32[]{:S(2)}) collective-permute-start(bf16[128,128]{1,0:T(8,128)(2,1)S(1)} %get-tuple-element.7), channel_id=1, source_target_pairs={{32,0},{64,32},{96,64},{128,96},{160,128},{192,160},{224,192},{33,... | collective-permute-start | bytes 98312 | tf_op jit(solution)/shard_map/ppermute | solution.py:274
  2.1 28.8 %collective-permute-start = (bf16[128,128]{1,0:T(8,128)(2,1)S(1)}, bf16[128,128]{1,0:T(8,128)(2,1)S(1)}, u32[]{:S(2)}, u32[]{:S(2)}) collective-permute-start(bf16[128,128]{1,0:T(8,128)(2,1)S(1)} %get-tuple-element.8), channel_id=1, source_target_pairs={{0,32},{32,64},{64,96},{96,128},{128,160},{160,192},{192,224},{1,3... | collective-permute-start | bytes 98312 | tf_op jit(solution)/shard_map/ppermute | solution.py:274
  6.3 24.6 %collective-permute-start.2 = (bf16[128,128]{1,0:T(8,128)(2,1)S(1)}, bf16[128,128]{1,0:T(8,128)(2,1)S(1)}, u32[]{:S(2)}, u32[]{:S(2)}) collective-permute-start(bf16[128,128]{1,0:T(8,128)(2,1)S(1)} %bitcast.17), channel_id=1, source_target_pairs={{0,1},{1,2},{2,3},{3,4},{4,5},{5,6},{6,7},{7,8},{8,9},{9,10},{10,1... | collective-permute-start | bytes 98312 | tf_op jit(solution)/shard_map/ppermute | solution.py:274
  9.7 21.2 %collective-permute-start.3 = (bf16[128,128]{1,0:T(8,128)(2,1)S(1)}, bf16[128,128]{1,0:T(8,128)(2,1)S(1)}, u32[]{:S(2)}, u32[]{:S(2)}) collective-permute-start(bf16[128,128]{1,0:T(8,128)(2,1)S(1)} %bitcast.18), channel_id=1, source_target_pairs={{1,0},{2,1},{3,2},{4,3},{5,4},{6,5},{7,6},{8,7},{9,8},{10,9},{11,1... | collective-permute-start | bytes 98312 | tf_op jit(solution)/shard_map/ppermute | solution.py:274
  12.1 2.2 %copy-start = (bf16[128,128,128]{2,1,0:T(8,128)(2,1)S(1)}, bf16[128,128,128]{2,1,0:T(8,128)(2,1)}, u32[]{:S(2)}) copy-start(bf16[128,128,128]{2,1,0:T(8,128)(2,1)} %refs_3_.3) | copy-start | bytes 12582916
  14.3 0.7 copy-start.2
  15.1 0.7 copy-start.3
  15.7 0.7 copy-start.4
  16.4 14.5 %copy-start.1 = (bf16[128,128,128]{2,1,0:T(8,128)(2,1)S(1)}, bf16[128,128,128]{2,1,0:T(8,128)(2,1)}, u32[]{:S(2)}) copy-start(bf16[128,128,128]{2,1,0:T(8,128)(2,1)} %refs_3_.3) | copy-start | bytes 12582916

commit v3 on v0

v3 whole, which is shorter than its diff:
```python
import jax
import jax.numpy as jnp
from jax import lax
from jax.experimental import pallas as pl
from jax.experimental.pallas import tpu as pltpu
from jax.sharding import PartitionSpec as P

BX = 16
LOG2E = 1.4426950408889634
CODE_TOP = 65535.0
CODE_STEP = CODE_TOP / 24.0
PREPARE_LIMIT = 24 * 1024 * 1024
RENDER_LIMIT = 24 * 1024 * 1024


def difference_matrix(rows):
    row = lax.broadcasted_iota(jnp.int32, (rows, rows), 0)
    col = lax.broadcasted_iota(jnp.int32, (rows, rows), 1)
    ahead = (row == col + 1).astype(jnp.float32)
    behind = (row + 1 == col).astype(jnp.float32)
    return (ahead - behind).astype(jnp.bfloat16)


def occupied_row(occ, zb, xb, rows, scale):
    parts = occ.shape[1]
    lane = lax.broadcasted_iota(jnp.int32, (BX, rows), 1)
    value = jnp.broadcast_to(occ[zb, parts - 1, xb], (BX, rows))
    for part in range(parts - 2, -1, -1):
        value = jnp.where(lane < (part + 1) * (rows // parts), occ[zb, part, xb], value)
    return value.astype(jnp.float32) * scale


def prepare_kernel(density, field, slope, diff):
    planes, columns, rows = density.shape
    diff[...] = difference_matrix(rows)

    @pl.loop(0, planes // 4)
    def _(k):
        at = pl.ds(4 * k, 4)
        part = density[at]
        field[at, 8:8 + columns, :] = part.astype(jnp.float32)
        step = jnp.dot(part.reshape(4 * columns, rows), diff[...],
                       preferred_element_type=jnp.float32)
        slope[at] = step.reshape(4, columns, rows)


def prepare(density):
    planes, columns, rows = density.shape
    vmem = pl.BlockSpec(memory_space=pltpu.VMEM)
    return pl.pallas_call(
        prepare_kernel,
        in_specs=[vmem],
        out_specs=[vmem] * 2,
        out_shape=[
            jax.ShapeDtypeStruct((planes, columns + 16, rows), jnp.float32),
            jax.ShapeDtypeStruct(density.shape, jnp.float32),
        ],
        scratch_shapes=[pltpu.VMEM((rows, rows), jnp.bfloat16)],
        cost_estimate=pl.CostEstimate(
            flops=2 * density.size * rows, bytes_accessed=10 * density.size, transcendentals=0
        ),
        compiler_params=pltpu.CompilerParams(vmem_limit_bytes=PREPARE_LIMIT),
    )(density)


def render_kernel(depth_scale, light_dir, pal, occ, field, slope, zlow, zhigh, xlow, xhigh,
                  out, edge, image):
    planes, columns, rows = slope.shape
    group = planes // occ.shape[0]
    f32 = jnp.float32
    edge[0] = xlow[...].astype(f32)
    edge[1] = xhigh[...].astype(f32)
    sublane = lax.broadcasted_iota(jnp.int32, (BX, rows), 0)
    light = [light_dir[i] for i in range(3)]
    half = [(0.5 * pal[0, c], 0.5 * pal[1, c]) for c in range(3)]
    extinct = (pal[0, 3] * LOG2E, pal[1, 3] * LOG2E)
    span = 2 * group
    steps = planes // span

    def march(block, outer):
        first = pl.multiple_of(block * BX, BX)
        lowest = (sublane == 0) & (block == 0)
        highest = (sublane == BX - 1) & (block != 0)

        def body(k, carry):
            total, through, red, green, blue, white = carry
            base = (steps - 1 - k) * span
            for zi in range(span - 1, -1, -1):
                if (zi + 1) % group == 0:
                    zb = base // group + zi // group
                    scale = occupied_row(occ, zb, block, rows, depth_scale)
                z = base + zi
                v = field[z, pl.ds(first + 8, BX), :]
                if zi == span - 1:
                    ahead = field[jnp.minimum(z + 1, planes - 1), pl.ds(first + 8, BX), :]
                    ahead = jnp.where(k == 0, zhigh[pl.ds(first, BX), :].astype(f32), ahead)
                else:
                    ahead = field[z + 1, pl.ds(first + 8, BX), :]
                if zi == 0:
                    behind = field[jnp.maximum(z - 1, 0), pl.ds(first + 8, BX), :]
                    ghost = zlow[pl.ds(first, BX), :].astype(f32)
                    behind = jnp.where(k == steps - 1, ghost, behind)
                else:
                    behind = field[z - 1, pl.ds(first + 8, BX), :]
                right = field[z, pl.ds(first + 9, BX), :]
                left = field[z, pl.ds(first + 7, BX), :]
                if outer:
                    right = jnp.where(highest, edge[1, pl.ds(z, 1), :], right)
                    left = jnp.where(lowest, edge[0, pl.ds(z, 1), :], left)
                gz = ahead - behind
                gx = right - left
                gy = slope[z, pl.ds(first, BX), :]
                norm = lax.rsqrt((gz * gz + gx * gx) + (gy * gy + 4.0))
                facing = (gz * light[0] + gx * light[1]) + gy * light[2]
                shade = jnp.abs(jnp.tanh(facing * norm)) + 3.0 / 7.0
                optical = jnp.log2(1.0 + jnp.exp2(v * extinct[0] + extinct[1]))
                total = total + scale * optical
                beyond = jnp.exp2(total)
                weight = (through - beyond) * shade
                through = beyond
                red = red + weight * jnp.tanh(v * half[0][0] + half[0][1])
                green = green + weight * jnp.tanh(v * half[1][0] + half[1][1])
                blue = blue + weight * jnp.tanh(v * half[2][0] + half[2][1])
                white = white + weight
            return total, through, red, green, blue, white

        zero = jnp.zeros((BX, rows), f32)
        total, _, red, green, blue, white = lax.fori_loop(
            0, steps, body, (zero, zero + 1.0, zero, zero, zero, zero)
        )
        at = pl.ds(first, BX)
        image[0, at, :] = 0.35 * (white + red)
        image[1, at, :] = 0.35 * (white + green)
        image[2, at, :] = 0.35 * (white + blue)
        image[3, at, :] = total

    last = columns // BX - 1

    @pl.loop(0, 2)
    def _(side):
        march(side * last, True)

    @pl.loop(1, last)
    def _(block):
        march(block, False)

    slabs, _, share, _ = out.shape
    for c in range(4):
        turned = image[c].T
        for d in range(slabs):
            out[d, c] = turned[d * share:(d + 1) * share, :]


def render(prepared, occ, light_dir, pal, halos, depth_scale, slabs):
    field, slope = prepared
    planes, columns, rows = slope.shape
    smem = pl.BlockSpec(memory_space=pltpu.SMEM)
    vmem = pl.BlockSpec(memory_space=pltpu.VMEM)
    return pl.pallas_call(
        lambda *refs: render_kernel(depth_scale, *refs),
        in_specs=[smem] * 3 + [vmem] * 6,
        out_specs=vmem,
        out_shape=jax.ShapeDtypeStruct((slabs, 4, rows // slabs, columns), jnp.float32),
        scratch_shapes=[
            pltpu.VMEM((2, planes, rows), jnp.float32),
            pltpu.VMEM((4, columns, rows), jnp.float32),
        ],
        compiler_params=pltpu.CompilerParams(vmem_limit_bytes=RENDER_LIMIT),
    )(light_dir, pal, occ, field, slope, *halos)


def composite(parts):
    slabs = parts.shape[0]
    colours, total = parts[slabs - 1, :3], parts[slabs - 1, 3:]
    for d in range(slabs - 2, -1, -1):
        colours = colours + jnp.exp2(total) * parts[d, :3]
        total = total + parts[d, 3:]
    return jnp.concatenate([colours, 1.0 - jnp.exp2(total)], axis=0)


def encode(pixels):
    level = jnp.log2(jnp.maximum(pixels, 2.0 ** -24))
    code = (level * CODE_STEP + (CODE_TOP + 0.5)).astype(jnp.int32) - 32768
    return code.astype(jnp.int16)


def decode(codes):
    code = codes.astype(jnp.float32)
    level = code * (1.0 / CODE_STEP) + (32768.0 - CODE_TOP) / CODE_STEP
    return jnp.where(code > -32768.0, jnp.exp2(level), 0.0)


def neighbours(axis, low, high):
    size = lax.axis_size(axis)
    up = [(i, i + 1) for i in range(size - 1)]
    down = [(j, i) for i, j in up]
    return lax.ppermute(high, axis, up), lax.ppermute(low, axis, down)


def local(density, occupancy, light_dir, palette):
    planes, columns, rows = density.shape
    slabs = lax.axis_size("depth")
    devices = lax.axis_size("cols")
    zhalo = neighbours("depth", density[0], density[-1])
    xhalo = neighbours("cols", density[:, 0, :], density[:, -1, :])
    occ = occupancy.transpose(0, 2, 1)
    depth_scale = -3.0 / (planes * slabs)
    parts = render(prepare(density), occ, light_dir, palette.T, zhalo + xhalo, depth_scale, slabs)
    parts = lax.all_to_all(parts, "depth", 0, 0, tiled=True)
    codes = encode(composite(parts))
    codes = jnp.broadcast_to(codes[None], (devices,) + codes.shape)
    codes = lax.all_to_all(codes, "cols", 0, 0, tiled=True)
    return decode(codes).transpose(1, 0, 3, 2).reshape(4, devices * columns, rows // slabs)


def solution(mesh):
    placed = (P("depth", "cols", None), P("depth", "cols", None), P(), P())
    return jax.shard_map(
        local, mesh=mesh, in_specs=placed, out_specs=P(None, None, "depth"), check_vma=False
    )
```

time: 290 us -> 76.2 us (0.26)
  local copies, waits for them, and re-layouts: 96.7 us -> 4.28 us
  waiting for transfers between devices: 83.5 us -> 0.01 us
  matrix products: 43.2 us -> 0 us
  blocking collectives: 0 us -> 40.7 us
  other arithmetic: 33.4 us -> 1.44 us
  Pallas kernels: 0 us -> 19.1 us
  between operations: 15.6 us -> 0.17 us
  starting transfers between devices: 16.2 us -> 10.2 us
    mul x5 -> x0, local copies, waits for them, and re-layouts: 87.5 us -> none  [the longest x4 78.5 us: expand_cells(): shaped * occ.astype(jnp.float32)[:, None, :, None, :, None]]
    all_gather x1 -> x0, waiting for transfers between devices: 74.7 us -> none  [local(): return lax.all_gather(pixels, 'cols', axis=1, tiled=True)]
    dot_general x1 -> x0, matrix products: 43.2 us -> none  [local(): jnp.dot(in_front, optical.reshape(planes, columns * rows), precision=lax....]
    all_to_all x0 -> x2, blocking collectives: none -> 40.7 us  [the longest x1 28.8 us: local(): codes = lax.all_to_all(codes, 'cols', 0, 0, tiled=True)]
    pallas_call x0 -> x2, Pallas kernels: none -> 19.1 us  [the longest x1 13.6 us: render(): pl.pallas_call(lambda *refs: render_kernel(depth_scale, *refs), in_specs=...]
    reduce_sum x1 -> x0, other arithmetic: 17.9 us -> none  [local(): channels.append(jnp.sum(optical, axis=0))]
    mul x4 -> x0, other arithmetic: 9.79 us -> none  [the longest x1 9.76 us: expand_cells(): shaped * occ.astype(jnp.float32)[:, None, :, None, :, None]]
    ppermute x7 -> x4, waiting for transfers between devices: 8.79 us -> 0.01 us  [neighbours(): return (lax.ppermute(high, axis, up), lax.ppermute(low, axis, down))]
  transfers between devices with their start and end apart: 8 -> 4, of which waited for: 5 -> 0; matrix products, arithmetic and copies ran while one was open for 28% -> 2% of each run, Pallas kernels for 0% -> 7%
where the time goes in v3:
time: 76.2 us; the launch traced here: 75.8 us
  blocking collectives  40.7 us (53%)
  Pallas kernels  19.1 us (25%)
  starting transfers between devices  10.2 us (13%)
  local copies, waits for them, and re-layouts  4.28 us (6%)
  other arithmetic  1.44 us (2%)
    all_to_all x1, blocking collectives, local(): codes = lax.all_to_all(codes, 'cols', 0, 0, tiled=True)  28.8 us
    pallas_call x1, Pallas kernels, render(): pl.pallas_call(lambda *refs: render_kernel(depth_scale, *refs), in_specs=...  13.6 us
    all_to_all x1, blocking collectives, local(): parts = lax.all_to_all(parts, 'depth', 0, 0, tiled=True)  11.9 us
    ppermute x4, starting transfers between devices, neighbours(): return (lax.ppermute(high, axis, up), lax.ppermute(low, axis, down))  10.2 us
    pallas_call x1, Pallas kernels, prepare(): pl.pallas_call(prepare_kernel, in_specs=[vmem], out_specs=[vmem] * 2, out...  5.47 us
    unnamed x10, local copies, waits for them, and re-layouts  2.21 us
  transfers between devices with their start and end apart: 4, of which 0 were waited for; matrix products, arithmetic and copies ran while one was open for 2% of the time, Pallas kernels for 7%

profile of v3, /device:TPU:2, one launch (start us, length us, event | category | flops | bytes accessed | tf_op | source)
XLA Modules:
  0.0 75.8 jit_solution(7426858195226607859)
XLA Ops:
  0.0 0.0 copy-start.2
  0.0 0.0 copy-start.3
  0.0 0.0 copy-start.1
  0.0 0.8 %slice_bitcast_fusion = (bf16[128,128]{1,0:T(8,128)(2,1)S(1)}, bf16[128,128]{1,0:T(8,128)(2,1)S(1)}) fusion(bf16[128,128,128]{2,1,0:T(8,128)(2,1)} %density.1), kind=kLoop, calls=%fused_computation.17 | loop fusion | bytes 131072 | tf_op jit(solution)/shard_map/squeeze | solution.py:204
  0.8 1.3 %collective-permute-start.1 = (bf16[128,128]{1,0:T(8,128)(2,1)S(1)}, bf16[128,128]{1,0:T(8,128)(2,1)S(1)}, u32[]{:S(2)}, u32[]{:S(2)}) collective-permute-start(bf16[128,128]{1,0:T(8,128)(2,1)S(1)} %get-tuple-element.15), channel_id=1, source_target_pairs={{32,0},{64,32},{96,64},{128,96},{160,128},{192,160},{224,192},{33,... | collective-permute-start | bytes 98312 | tf_op jit(solution)/shard_map/ppermute | solution.py:197
  2.1 3.0 %collective-permute-start = (bf16[128,128]{1,0:T(8,128)(2,1)S(1)}, bf16[128,128]{1,0:T(8,128)(2,1)S(1)}, u32[]{:S(2)}, u32[]{:S(2)}) collective-permute-start(bf16[128,128]{1,0:T(8,128)(2,1)S(1)} %get-tuple-element.16), channel_id=1, source_target_pairs={{0,32},{32,64},{64,96},{96,128},{128,160},{160,192},{192,224},{1,3... | collective-permute-start | bytes 98312 | tf_op jit(solution)/shard_map/ppermute | solution.py:197
  5.2 1.1 %fusion.23 = (bf16[128,1,128]{2,1,0:T(2,128)(2,1)S(1)}, bf16[128,1,128]{2,1,0:T(2,128)(2,1)S(1)}) fusion(bf16[128,128,128]{2,1,0:T(8,128)(2,1)} %density.1), kind=kLoop, calls=%fused_computation.52 | loop fusion | bytes 131072 | tf_op jit(solution)/shard_map/slice | solution.py:205
  6.3 3.4 %collective-permute-start.2 = (bf16[128,128]{1,0:T(8,128)(2,1)S(1)}, bf16[128,128]{1,0:T(8,128)(2,1)S(1)}, u32[]{:S(2)}, u32[]{:S(2)}) collective-permute-start(bf16[128,128]{1,0:T(8,128)(2,1)S(1)} %bitcast.38), channel_id=1, source_target_pairs={{0,1},{1,2},{2,3},{3,4},{4,5},{5,6},{6,7},{7,8},{8,9},{9,10},{10,1... | collective-permute-start | bytes 98312 | tf_op jit(solution)/shard_map/ppermute | solution.py:197
  9.7 2.4 %collective-permute-start.3 = (bf16[128,128]{1,0:T(8,128)(2,1)S(1)}, bf16[128,128]{1,0:T(8,128)(2,1)S(1)}, u32[]{:S(2)}, u32[]{:S(2)}) collective-permute-start(bf16[128,128]{1,0:T(8,128)(2,1)S(1)} %bitcast.39), channel_id=1, source_target_pairs={{1,0},{2,1},{3,2},{4,3},{5,4},{6,5},{7,6},{8,7},{9,8},{10,9},{11,1... | collective-permute-start | bytes 98312 | tf_op jit(solution)/shard_map/ppermute | solution.py:197
  12.2 0.0 copy-start
  12.2 2.2 %copy-done = bf16[128,128,128]{2,1,0:T(8,128)(2,1)S(1)} copy-done((bf16[128,128,128]{2,1,0:T(8,128)(2,1)S(1)}, bf16[128,128,128]{2,1,0:T(8,128)(2,1)}, u32[]{:S(2)}) %copy-start) | copy-done | bytes 4194328
  14.4 5.5 %shard_map.46 = (f32[128,144,128]{2,1,0:T(8,128)S(1)}, f32[128,128,128]{2,1,0:T(8,128)S(1)}) custom-call(bf16[128,128,128]{2,1,0:T(8,128)(2,1)S(1)} %copy-done), custom_call_target="tpu_custom_call" | custom-call | flops 536870912 | bytes 20971520 | tf_op jit(solution)/shard_map/pallas_call | solution.py:50
  19.9 0.0 collective-permute-done.1.refs_6_
  19.9 0.0 collective-permute-done.refs_5_
  19.9 0.0 collective-permute-done.2.refs_7_
  19.9 0.0 collective-permute-done.3.refs_8_
  19.9 0.0 copy-done.2
  19.9 0.0 copy-done.3
  19.9 0.0 copy-done.1
  19.9 13.6 %shard_map.47 = f32[8,4,16,128]{3,2,1,0:T(8,128)S(1)} custom-call(f32[3]{0:T(128)S(1)} %copy-done.3, f32[2,4]{1,0:T(2,128)S(1)} %bitcast.37, s32[8,4,8]{2,1,0:T(4,128)S(1)} %bitcast.36, f32[128,144,128]{2,1,0:T(8,128)S(1)} %get-tuple-element.7.refs_3_, f32[128,128,128]{2,1,0:T(8,128)S(1)} %get-tuple-element.8.refs_4_, ...), custom_call_target="tpu_custom_call" | custom-call | tf_op jit(solution)/shard_map/pallas_call | solution.py:159
  33.6 11.9 %all_to_all.10 = f32[8,4,16,128]{3,2,1,0:T(8,128)S(1)} all-to-all(f32[8,4,16,128]{3,2,1,0:T(8,128)S(1)} %shard_map.47), channel_id=1, replica_groups=mesh['depth'=8,'cols'=32] {'depth'}, dimensions={0} | all-to-all | bytes 524288 | tf_op jit(solution)/shard_map/all_to_all | solution.py:209
  45.6 0.1 broadcast_in_dim.10
  45.7 28.8 %all_to_all.11 = s16[32,4,16,128]{3,2,1,0:T(8,128)(2,1)S(1)} all-to-all(s16[32,4,16,128]{3,2,1,0:T(8,128)(2,1)S(1)} %broadcast_in_dim.10), channel_id=1, replica_groups=mesh['depth'=8,'cols'=32] {'cols'}, dimensions={0} | all-to-all | bytes 1048576 | tf_op jit(solution)/shard_map/all_to_all | solution.py:212
  74.5 1.3 %copy_bitcast_fusion = f32[4,4096,16]{1,2,0:T(8,128)} fusion(s16[32,4,16,128]{3,2,1,0:T(8,128)(2,1)S(1)} %all_to_all.11), kind=kLoop, calls=%fused_computation.7 | loop fusion | flops 1572864 | bytes 1572864 | tf_op jit(solution)/shard_map/reshape | solution.py:213
  (7 shorter events, 0.1 us)
Async XLA Ops:
  0.0 19.9 %copy-start.2 = (f32[4,2]{0,1:T(2,128)S(1)}, f32[4,2]{0,1:T(2,128)}, u32[]{:S(2)}) copy-start(f32[4,2]{0,1:T(2,128)} %param.7) | copy-start | bytes 100
  0.0 19.9 %copy-start.3 = (f32[3]{0:T(128)S(1)}, f32[3]{0:T(128)}, u32[]{:S(2)}) copy-start(f32[3]{0:T(128)} %refs_0_.1) | copy-start | bytes 40
  0.0 19.9 %copy-start.1 = (s32[8,8,4]{1,2,0:T(4,128)S(1)}, s32[8,8,4]{1,2,0:T(4,128)}, u32[]{:S(2)}) copy-start(s32[8,8,4]{1,2,0:T(4,128)} %param.5) | copy-start | bytes 3076
  0.8 19.0 %collective-permute-start.1 = (bf16[128,128]{1,0:T(8,128)(2,1)S(1)}, bf16[128,128]{1,0:T(8,128)(2,1)S(1)}, u32[]{:S(2)}, u32[]{:S(2)}) collective-permute-start(bf16[128,128]{1,0:T(8,128)(2,1)S(1)} %get-tuple-element.15), channel_id=1, source_target_pairs={{32,0},{64,32},{96,64},{128,96},{160,128},{192,160},{224,192},{33,... | collective-permute-start | bytes 98312 | tf_op jit(solution)/shard_map/ppermute | solution.py:197
  2.1 17.8 %collective-permute-start = (bf16[128,128]{1,0:T(8,128)(2,1)S(1)}, bf16[128,128]{1,0:T(8,128)(2,1)S(1)}, u32[]{:S(2)}, u32[]{:S(2)}) collective-permute-start(bf16[128,128]{1,0:T(8,128)(2,1)S(1)} %get-tuple-element.16), channel_id=1, source_target_pairs={{0,32},{32,64},{64,96},{96,128},{128,160},{160,192},{192,224},{1,3... | collective-permute-start | bytes 98312 | tf_op jit(solution)/shard_map/ppermute | solution.py:197
  6.3 13.6 %collective-permute-start.2 = (bf16[128,128]{1,0:T(8,128)(2,1)S(1)}, bf16[128,128]{1,0:T(8,128)(2,1)S(1)}, u32[]{:S(2)}, u32[]{:S(2)}) collective-permute-start(bf16[128,128]{1,0:T(8,128)(2,1)S(1)} %bitcast.38), channel_id=1, source_target_pairs={{0,1},{1,2},{2,3},{3,4},{4,5},{5,6},{6,7},{7,8},{8,9},{9,10},{10,1... | collective-permute-start | bytes 98312 | tf_op jit(solution)/shard_map/ppermute | solution.py:197
  9.7 10.2 %collective-permute-start.3 = (bf16[128,128]{1,0:T(8,128)(2,1)S(1)}, bf16[128,128]{1,0:T(8,128)(2,1)S(1)}, u32[]{:S(2)}, u32[]{:S(2)}) collective-permute-start(bf16[128,128]{1,0:T(8,128)(2,1)S(1)} %bitcast.39), channel_id=1, source_target_pairs={{1,0},{2,1},{3,2},{4,3},{5,4},{6,5},{7,6},{8,7},{9,8},{10,9},{11,1... | collective-permute-start | bytes 98312 | tf_op jit(solution)/shard_map/ppermute | solution.py:197
  12.2 2.2 %copy-start = (bf16[128,128,128]{2,1,0:T(8,128)(2,1)S(1)}, bf16[128,128,128]{2,1,0:T(8,128)(2,1)}, u32[]{:S(2)}) copy-start(bf16[128,128,128]{2,1,0:T(8,128)(2,1)} %density.1) | copy-start | bytes 12582916

commit v4 on v3

--- a/solution.py
+++ b/solution.py
@@ -34,14 +34,14 @@
     planes, columns, rows = density.shape
     diff[...] = difference_matrix(rows)
 
-    @pl.loop(0, planes // 4)
+    @pl.loop(0, planes // 16)
     def _(k):
-        at = pl.ds(4 * k, 4)
+        at = pl.ds(16 * k, 16)
         part = density[at]
         field[at, 8:8 + columns, :] = part.astype(jnp.float32)
-        step = jnp.dot(part.reshape(4 * columns, rows), diff[...],
+        step = jnp.dot(part.reshape(16 * columns, rows), diff[...],
                        preferred_element_type=jnp.float32)
-        slope[at] = step.reshape(4, columns, rows)
+        slope[at] = step.reshape(16, columns, rows)
 
 
 def prepare(density):

time: 76.2 us -> 73.1 us (0.959)
  Pallas kernels: 19.1 us -> 16 us
    pallas_call x1, Pallas kernels: 5.47 us -> 2.36 us  [prepare(): pl.pallas_call(prepare_kernel, in_specs=[vmem], out_specs=[vmem] * 2, out...]
  transfers between devices with their start and end apart: 4 -> 4, of which waited for: 0 -> 0; matrix products, arithmetic and copies ran while one was open for 2% -> 2% of each run, Pallas kernels for 7% -> 3%
where the time goes in v4:
time: 73.1 us; the launch traced here: 72.7 us
  blocking collectives  40.7 us (56%)
  Pallas kernels  16 us (22%)
  starting transfers between devices  10.2 us (14%)
  local copies, waits for them, and re-layouts  4.28 us (6%)
  other arithmetic  1.44 us (2%)
    all_to_all x1, blocking collectives, local(): codes = lax.all_to_all(codes, 'cols', 0, 0, tiled=True)  28.7 us
    pallas_call x1, Pallas kernels, render(): pl.pallas_call(lambda *refs: render_kernel(depth_scale, *refs), in_specs=...  13.6 us
    all_to_all x1, blocking collectives, local(): parts = lax.all_to_all(parts, 'depth', 0, 0, tiled=True)  11.9 us
    ppermute x4, starting transfers between devices, neighbours(): return (lax.ppermute(high, axis, up), lax.ppermute(low, axis, down))  10.2 us
    pallas_call x1, Pallas kernels, prepare(): pl.pallas_call(prepare_kernel, in_specs=[vmem], out_specs=[vmem] * 2, out...  2.36 us
    unnamed x10, local copies, waits for them, and re-layouts  2.21 us
  transfers between devices with their start and end apart: 4, of which 0 were waited for; matrix products, arithmetic and copies ran while one was open for 2% of the time, Pallas kernels for 3%

profile of v4, /device:TPU:2, one launch (start us, length us, event | category | flops | bytes accessed | tf_op | source)
XLA Modules:
  0.0 72.7 jit_solution(16419361309846853932)
XLA Ops:
  0.0 0.0 copy-start.2
  0.0 0.0 copy-start.3
  0.0 0.0 copy-start.1
  0.0 0.8 %slice_bitcast_fusion = (bf16[128,128]{1,0:T(8,128)(2,1)S(1)}, bf16[128,128]{1,0:T(8,128)(2,1)S(1)}) fusion(bf16[128,128,128]{2,1,0:T(8,128)(2,1)} %density.1), kind=kLoop, calls=%fused_computation.17 | loop fusion | bytes 131072 | tf_op jit(solution)/shard_map/squeeze | solution.py:204
  0.8 1.3 %collective-permute-start.1 = (bf16[128,128]{1,0:T(8,128)(2,1)S(1)}, bf16[128,128]{1,0:T(8,128)(2,1)S(1)}, u32[]{:S(2)}, u32[]{:S(2)}) collective-permute-start(bf16[128,128]{1,0:T(8,128)(2,1)S(1)} %get-tuple-element.15), channel_id=1, source_target_pairs={{32,0},{64,32},{96,64},{128,96},{160,128},{192,160},{224,192},{33,... | collective-permute-start | bytes 98312 | tf_op jit(solution)/shard_map/ppermute | solution.py:197
  2.1 3.0 %collective-permute-start = (bf16[128,128]{1,0:T(8,128)(2,1)S(1)}, bf16[128,128]{1,0:T(8,128)(2,1)S(1)}, u32[]{:S(2)}, u32[]{:S(2)}) collective-permute-start(bf16[128,128]{1,0:T(8,128)(2,1)S(1)} %get-tuple-element.16), channel_id=1, source_target_pairs={{0,32},{32,64},{64,96},{96,128},{128,160},{160,192},{192,224},{1,3... | collective-permute-start | bytes 98312 | tf_op jit(solution)/shard_map/ppermute | solution.py:197
  5.2 1.1 %fusion.23 = (bf16[128,1,128]{2,1,0:T(2,128)(2,1)S(1)}, bf16[128,1,128]{2,1,0:T(2,128)(2,1)S(1)}) fusion(bf16[128,128,128]{2,1,0:T(8,128)(2,1)} %density.1), kind=kLoop, calls=%fused_computation.52 | loop fusion | bytes 131072 | tf_op jit(solution)/shard_map/slice | solution.py:205
  6.3 3.4 %collective-permute-start.2 = (bf16[128,128]{1,0:T(8,128)(2,1)S(1)}, bf16[128,128]{1,0:T(8,128)(2,1)S(1)}, u32[]{:S(2)}, u32[]{:S(2)}) collective-permute-start(bf16[128,128]{1,0:T(8,128)(2,1)S(1)} %bitcast.38), channel_id=1, source_target_pairs={{0,1},{1,2},{2,3},{3,4},{4,5},{5,6},{6,7},{7,8},{8,9},{9,10},{10,1... | collective-permute-start | bytes 98312 | tf_op jit(solution)/shard_map/ppermute | solution.py:197
  9.7 2.4 %collective-permute-start.3 = (bf16[128,128]{1,0:T(8,128)(2,1)S(1)}, bf16[128,128]{1,0:T(8,128)(2,1)S(1)}, u32[]{:S(2)}, u32[]{:S(2)}) collective-permute-start(bf16[128,128]{1,0:T(8,128)(2,1)S(1)} %bitcast.39), channel_id=1, source_target_pairs={{1,0},{2,1},{3,2},{4,3},{5,4},{6,5},{7,6},{8,7},{9,8},{10,9},{11,1... | collective-permute-start | bytes 98312 | tf_op jit(solution)/shard_map/ppermute | solution.py:197
  12.2 0.0 copy-start
  12.2 2.2 %copy-done = bf16[128,128,128]{2,1,0:T(8,128)(2,1)S(1)} copy-done((bf16[128,128,128]{2,1,0:T(8,128)(2,1)S(1)}, bf16[128,128,128]{2,1,0:T(8,128)(2,1)}, u32[]{:S(2)}) %copy-start) | copy-done | bytes 4194328
  14.4 2.4 %shard_map.46 = (f32[128,144,128]{2,1,0:T(8,128)S(1)}, f32[128,128,128]{2,1,0:T(8,128)S(1)}) custom-call(bf16[128,128,128]{2,1,0:T(8,128)(2,1)S(1)} %copy-done), custom_call_target="tpu_custom_call" | custom-call | flops 536870912 | bytes 20971520 | tf_op jit(solution)/shard_map/pallas_call | solution.py:50
  16.7 0.0 collective-permute-done.1.refs_6_
  16.8 0.0 collective-permute-done.refs_5_
  16.8 0.0 collective-permute-done.2.refs_7_
  16.8 0.0 collective-permute-done.3.refs_8_
  16.8 0.0 copy-done.2
  16.8 0.0 copy-done.3
  16.8 0.0 copy-done.1
  16.8 13.6 %shard_map.47 = f32[8,4,16,128]{3,2,1,0:T(8,128)S(1)} custom-call(f32[3]{0:T(128)S(1)} %copy-done.3, f32[2,4]{1,0:T(2,128)S(1)} %bitcast.37, s32[8,4,8]{2,1,0:T(4,128)S(1)} %bitcast.36, f32[128,144,128]{2,1,0:T(8,128)S(1)} %get-tuple-element.7.refs_3_, f32[128,128,128]{2,1,0:T(8,128)S(1)} %get-tuple-element.8.refs_4_, ...), custom_call_target="tpu_custom_call" | custom-call | tf_op jit(solution)/shard_map/pallas_call | solution.py:159
  30.4 11.9 %all_to_all.10 = f32[8,4,16,128]{3,2,1,0:T(8,128)S(1)} all-to-all(f32[8,4,16,128]{3,2,1,0:T(8,128)S(1)} %shard_map.47), channel_id=1, replica_groups=mesh['depth'=8,'cols'=32] {'depth'}, dimensions={0} | all-to-all | bytes 524288 | tf_op jit(solution)/shard_map/all_to_all | solution.py:209
  42.5 0.1 broadcast_in_dim.10
  42.6 28.7 %all_to_all.11 = s16[32,4,16,128]{3,2,1,0:T(8,128)(2,1)S(1)} all-to-all(s16[32,4,16,128]{3,2,1,0:T(8,128)(2,1)S(1)} %broadcast_in_dim.10), channel_id=1, replica_groups=mesh['depth'=8,'cols'=32] {'cols'}, dimensions={0} | all-to-all | bytes 1048576 | tf_op jit(solution)/shard_map/all_to_all | solution.py:212
  71.3 1.3 %copy_bitcast_fusion = f32[4,4096,16]{1,2,0:T(8,128)} fusion(s16[32,4,16,128]{3,2,1,0:T(8,128)(2,1)S(1)} %all_to_all.11), kind=kLoop, calls=%fused_computation.7 | loop fusion | flops 1572864 | bytes 1572864 | tf_op jit(solution)/shard_map/reshape | solution.py:213
  (7 shorter events, 0.1 us)
Async XLA Ops:
  0.0 16.8 %copy-start.2 = (f32[4,2]{0,1:T(2,128)S(1)}, f32[4,2]{0,1:T(2,128)}, u32[]{:S(2)}) copy-start(f32[4,2]{0,1:T(2,128)} %param.7) | copy-start | bytes 100
  0.0 16.8 %copy-start.3 = (f32[3]{0:T(128)S(1)}, f32[3]{0:T(128)}, u32[]{:S(2)}) copy-start(f32[3]{0:T(128)} %refs_0_.1) | copy-start | bytes 40
  0.0 16.8 %copy-start.1 = (s32[8,8,4]{1,2,0:T(4,128)S(1)}, s32[8,8,4]{1,2,0:T(4,128)}, u32[]{:S(2)}) copy-start(s32[8,8,4]{1,2,0:T(4,128)} %param.5) | copy-start | bytes 3076
  0.8 15.9 %collective-permute-start.1 = (bf16[128,128]{1,0:T(8,128)(2,1)S(1)}, bf16[128,128]{1,0:T(8,128)(2,1)S(1)}, u32[]{:S(2)}, u32[]{:S(2)}) collective-permute-start(bf16[128,128]{1,0:T(8,128)(2,1)S(1)} %get-tuple-element.15), channel_id=1, source_target_pairs={{32,0},{64,32},{96,64},{128,96},{160,128},{192,160},{224,192},{33,... | collective-permute-start | bytes 98312 | tf_op jit(solution)/shard_map/ppermute | solution.py:197
  2.1 14.6 %collective-permute-start = (bf16[128,128]{1,0:T(8,128)(2,1)S(1)}, bf16[128,128]{1,0:T(8,128)(2,1)S(1)}, u32[]{:S(2)}, u32[]{:S(2)}) collective-permute-start(bf16[128,128]{1,0:T(8,128)(2,1)S(1)} %get-tuple-element.16), channel_id=1, source_target_pairs={{0,32},{32,64},{64,96},{96,128},{128,160},{160,192},{192,224},{1,3... | collective-permute-start | bytes 98312 | tf_op jit(solution)/shard_map/ppermute | solution.py:197
  6.3 10.4 %collective-permute-start.2 = (bf16[128,128]{1,0:T(8,128)(2,1)S(1)}, bf16[128,128]{1,0:T(8,128)(2,1)S(1)}, u32[]{:S(2)}, u32[]{:S(2)}) collective-permute-start(bf16[128,128]{1,0:T(8,128)(2,1)S(1)} %bitcast.38), channel_id=1, source_target_pairs={{0,1},{1,2},{2,3},{3,4},{4,5},{5,6},{6,7},{7,8},{8,9},{9,10},{10,1... | collective-permute-start | bytes 98312 | tf_op jit(solution)/shard_map/ppermute | solution.py:197
  9.7 7.0 %collective-permute-start.3 = (bf16[128,128]{1,0:T(8,128)(2,1)S(1)}, bf16[128,128]{1,0:T(8,128)(2,1)S(1)}, u32[]{:S(2)}, u32[]{:S(2)}) collective-permute-start(bf16[128,128]{1,0:T(8,128)(2,1)S(1)} %bitcast.39), channel_id=1, source_target_pairs={{1,0},{2,1},{3,2},{4,3},{5,4},{6,5},{7,6},{8,7},{9,8},{10,9},{11,1... | collective-permute-start | bytes 98312 | tf_op jit(solution)/shard_map/ppermute | solution.py:197
  12.2 2.2 %copy-start = (bf16[128,128,128]{2,1,0:T(8,128)(2,1)S(1)}, bf16[128,128,128]{2,1,0:T(8,128)(2,1)}, u32[]{:S(2)}) copy-start(bf16[128,128,128]{2,1,0:T(8,128)(2,1)} %density.1) | copy-start | bytes 12582916

commit v5 on v4

--- a/solution.py
+++ b/solution.py
@@ -192,9 +192,12 @@
 
 def neighbours(axis, low, high):
     size = lax.axis_size(axis)
-    up = [(i, i + 1) for i in range(size - 1)]
-    down = [(j, i) for i, j in up]
-    return lax.ppermute(high, axis, up), lax.ppermute(low, axis, down)
+    odd = lax.axis_index(axis) % 2 == 1
+    near = [pair for i in range(0, size - 1, 2) for pair in ((i, i + 1), (i + 1, i))]
+    far = [pair for i in range(1, size - 1, 2) for pair in ((i, i + 1), (i + 1, i))]
+    from_far = lax.ppermute(jnp.where(odd, high, low), axis, far)
+    from_near = lax.ppermute(jnp.where(odd, low, high), axis, near)
+    return jnp.where(odd, from_near, from_far), jnp.where(odd, from_far, from_near)
 
 
 def local(density, occupancy, light_dir, palette):

time: 73.1 us -> 69.4 us (0.949)
  starting transfers between devices: 10.2 us -> 7.17 us
  local copies, waits for them, and re-layouts: 4.28 us -> 3.44 us
  other arithmetic: 1.44 us -> 2.28 us
    ppermute x4, starting transfers between devices: 10.2 us -> 7.17 us  [the longest x2 4.05 us: neighbours(): from_far = lax.ppermute(jnp.where(odd, high, low), axis, far)]
    select_n x0 -> x4, other arithmetic: none -> 0.84 us  [the longest x2 0.82 us: neighbours(): from_far = lax.ppermute(jnp.where(odd, high, low), axis, far)]
    squeeze x1 -> x0, local copies, waits for them, and re-layouts: 0.82 us -> none  [local(): zhalo = neighbours('depth', density[0], density[-1])]
    unnamed x10 -> x8, local copies, waits for them, and re-layouts: 2.21 us -> 2.19 us
where the time goes in v5:
time: 69.4 us; the launch traced here: 69.1 us
  blocking collectives  40 us (58%)
  Pallas kernels  16 us (23%)
  starting transfers between devices  7.17 us (10%)
  local copies, waits for them, and re-layouts  3.44 us (5%)
  other arithmetic  2.28 us (3%)
    all_to_all x1, blocking collectives, local(): codes = lax.all_to_all(codes, 'cols', 0, 0, tiled=True)  28.5 us
    pallas_call x1, Pallas kernels, render(): pl.pallas_call(lambda *refs: render_kernel(depth_scale, *refs), in_specs=...  13.6 us
    all_to_all x1, blocking collectives, local(): parts = lax.all_to_all(parts, 'depth', 0, 0, tiled=True)  11.5 us
    ppermute x2, starting transfers between devices, neighbours(): from_far = lax.ppermute(jnp.where(odd, high, low), axis, far)  4.05 us
    ppermute x2, starting transfers between devices, neighbours(): from_near = lax.ppermute(jnp.where(odd, low, high), axis, near)  3.12 us
    pallas_call x1, Pallas kernels, prepare(): pl.pallas_call(prepare_kernel, in_specs=[vmem], out_specs=[vmem] * 2, out...  2.36 us
    unnamed x8, local copies, waits for them, and re-layouts  2.19 us
  transfers between devices with their start and end apart: 4, of which 0 were waited for; matrix products, arithmetic and copies ran while one was open for 2% of the time, Pallas kernels for 3%

profile of v5, /device:TPU:2, one launch (start us, length us, event | category | flops | bytes accessed | tf_op | source)
XLA Modules:
  0.0 69.1 jit_solution(11907655712861605104)
XLA Ops:
  0.0 0.0 copy-start.2
  0.0 0.0 copy-start.3
  0.0 0.0 copy-start.1
  0.0 0.8 %select_bitcast_fusion.2 = (bf16[128,128]{1,0:T(8,128)(2,1)S(1)}, bf16[128,128]{1,0:T(8,128)(2,1)S(1)}) fusion(pred[]{:T(512)S(6)} %eq.9, bf16[128,128,128]{2,1,0:T(8,128)(2,1)} %density.1), kind=kLoop, calls=%fused_computation.17 | loop fusion | flops 32768 | bytes 131073 | tf_op jit(solution)/shard_map/jit(_where)/select_n | solution.py:198
  0.8 0.7 collective-permute-start.1
  1.5 3.0 %collective-permute-start = (bf16[128,128]{1,0:T(8,128)(2,1)S(1)}, bf16[128,128]{1,0:T(8,128)(2,1)S(1)}, u32[]{:S(2)}, u32[]{:S(2)}) collective-permute-start(bf16[128,128]{1,0:T(8,128)(2,1)S(1)} %get-tuple-element.16), channel_id=1, source_target_pairs={{0,32},{32,0},{64,96},{96,64},{128,160},{160,128},{192,224},{224,1... | collective-permute-start | bytes 98312 | tf_op jit(solution)/shard_map/ppermute | solution.py:199
  4.5 1.1 %fusion.23 = (bf16[128,1,128]{2,1,0:T(2,128)(2,1)S(1)}, bf16[128,1,128]{2,1,0:T(2,128)(2,1)S(1)}) fusion(bf16[128,128,128]{2,1,0:T(8,128)(2,1)} %density.1), kind=kLoop, calls=%fused_computation.56 | loop fusion | bytes 131072 | tf_op jit(solution)/shard_map/slice | solution.py:208
  5.7 3.4 %collective-permute-start.3 = (bf16[128,128]{1,0:T(8,128)(2,1)S(1)}, bf16[128,128]{1,0:T(8,128)(2,1)S(1)}, u32[]{:S(2)}, u32[]{:S(2)}) collective-permute-start(bf16[128,128]{1,0:T(8,128)(2,1)S(1)} %get-tuple-element.23), channel_id=1, source_target_pairs={{1,2},{2,1},{3,4},{4,3},{5,6},{6,5},{7,8},{8,7},{9,10},{10,9},{11,... | collective-permute-start | bytes 98312 | tf_op jit(solution)/shard_map/ppermute | solution.py:198
  9.1 0.1 collective-permute-start.2
  9.2 0.0 copy-start
  9.2 2.2 %copy-done = bf16[128,128,128]{2,1,0:T(8,128)(2,1)S(1)} copy-done((bf16[128,128,128]{2,1,0:T(8,128)(2,1)S(1)}, bf16[128,128,128]{2,1,0:T(8,128)(2,1)}, u32[]{:S(2)}) %copy-start) | copy-done | bytes 4194328
  11.4 2.4 %shard_map.46 = (f32[128,144,128]{2,1,0:T(8,128)S(1)}, f32[128,128,128]{2,1,0:T(8,128)S(1)}) custom-call(bf16[128,128,128]{2,1,0:T(8,128)(2,1)S(1)} %copy-done), custom_call_target="tpu_custom_call" | custom-call | flops 536870912 | bytes 20971520 | tf_op jit(solution)/shard_map/pallas_call | solution.py:50
  13.7 0.0 collective-permute-done.1
  13.8 0.0 collective-permute-done
  13.8 0.0 collective-permute-done.3
  13.8 0.0 collective-permute-done.2
  13.8 0.0 copy-done.2
  13.8 0.0 copy-done.3
  13.8 0.0 copy-done.1
  13.9 13.6 %shard_map.47 = f32[8,4,16,128]{3,2,1,0:T(8,128)S(1)} custom-call(f32[3]{0:T(128)S(1)} %copy-done.3, f32[2,4]{1,0:T(2,128)S(1)} %bitcast.35, s32[8,4,8]{2,1,0:T(4,128)S(1)} %bitcast.34, f32[128,144,128]{2,1,0:T(8,128)S(1)} %get-tuple-element.7.refs_3_, f32[128,128,128]{2,1,0:T(8,128)S(1)} %get-tuple-element.8.refs_4_, ...), custom_call_target="tpu_custom_call" | custom-call | tf_op jit(solution)/shard_map/pallas_call | solution.py:159
  27.5 11.5 %all_to_all.10 = f32[8,4,16,128]{3,2,1,0:T(8,128)S(1)} all-to-all(f32[8,4,16,128]{3,2,1,0:T(8,128)S(1)} %shard_map.47), channel_id=1, replica_groups=mesh['depth'=8,'cols'=32] {'depth'}, dimensions={0} | all-to-all | bytes 524288 | tf_op jit(solution)/shard_map/all_to_all | solution.py:212
  39.1 0.1 broadcast_in_dim.10
  39.2 28.5 %all_to_all.11 = s16[32,4,16,128]{3,2,1,0:T(8,128)(2,1)S(1)} all-to-all(s16[32,4,16,128]{3,2,1,0:T(8,128)(2,1)S(1)} %broadcast_in_dim.10), channel_id=1, replica_groups=mesh['depth'=8,'cols'=32] {'cols'}, dimensions={0} | all-to-all | bytes 1048576 | tf_op jit(solution)/shard_map/all_to_all | solution.py:215
  67.7 1.3 %copy_bitcast_fusion = f32[4,4096,16]{1,2,0:T(8,128)} fusion(s16[32,4,16,128]{3,2,1,0:T(8,128)(2,1)S(1)} %all_to_all.11), kind=kLoop, calls=%fused_computation.7 | loop fusion | flops 1572864 | bytes 1572864 | tf_op jit(solution)/shard_map/reshape | solution.py:216
  (8 shorter events, 0.1 us)
Async XLA Ops:
  0.0 13.8 %copy-start.2 = (f32[4,2]{0,1:T(2,128)S(1)}, f32[4,2]{0,1:T(2,128)}, u32[]{:S(2)}) copy-start(f32[4,2]{0,1:T(2,128)} %param.7) | copy-start | bytes 100
  0.0 13.8 %copy-start.3 = (f32[3]{0:T(128)S(1)}, f32[3]{0:T(128)}, u32[]{:S(2)}) copy-start(f32[3]{0:T(128)} %refs_0_.1) | copy-start | bytes 40
  0.0 13.8 %copy-start.1 = (s32[8,8,4]{1,2,0:T(4,128)S(1)}, s32[8,8,4]{1,2,0:T(4,128)}, u32[]{:S(2)}) copy-start(s32[8,8,4]{1,2,0:T(4,128)} %param.5) | copy-start | bytes 3076
  0.8 12.9 %collective-permute-start.1 = (bf16[128,128]{1,0:T(8,128)(2,1)S(1)}, bf16[128,128]{1,0:T(8,128)(2,1)S(1)}, u32[]{:S(2)}, u32[]{:S(2)}) collective-permute-start(bf16[128,128]{1,0:T(8,128)(2,1)S(1)} %get-tuple-element.15), channel_id=1, source_target_pairs={{32,64},{64,32},{96,128},{128,96},{160,192},{192,160},{33,65},{65,... | collective-permute-start | bytes 98312 | tf_op jit(solution)/shard_map/ppermute | solution.py:198
  1.5 12.3 %collective-permute-start = (bf16[128,128]{1,0:T(8,128)(2,1)S(1)}, bf16[128,128]{1,0:T(8,128)(2,1)S(1)}, u32[]{:S(2)}, u32[]{:S(2)}) collective-permute-start(bf16[128,128]{1,0:T(8,128)(2,1)S(1)} %get-tuple-element.16), channel_id=1, source_target_pairs={{0,32},{32,0},{64,96},{96,64},{128,160},{160,128},{192,224},{224,1... | collective-permute-start | bytes 98312 | tf_op jit(solution)/shard_map/ppermute | solution.py:199
  5.7 8.1 %collective-permute-start.3 = (bf16[128,128]{1,0:T(8,128)(2,1)S(1)}, bf16[128,128]{1,0:T(8,128)(2,1)S(1)}, u32[]{:S(2)}, u32[]{:S(2)}) collective-permute-start(bf16[128,128]{1,0:T(8,128)(2,1)S(1)} %get-tuple-element.23), channel_id=1, source_target_pairs={{1,2},{2,1},{3,4},{4,3},{5,6},{6,5},{7,8},{8,7},{9,10},{10,9},{11,... | collective-permute-start | bytes 98312 | tf_op jit(solution)/shard_map/ppermute | solution.py:198
  9.1 4.7 %collective-permute-start.2 = (bf16[128,128]{1,0:T(8,128)(2,1)S(1)}, bf16[128,128]{1,0:T(8,128)(2,1)S(1)}, u32[]{:S(2)}, u32[]{:S(2)}) collective-permute-start(bf16[128,128]{1,0:T(8,128)(2,1)S(1)} %get-tuple-element.24), channel_id=1, source_target_pairs={{0,1},{1,0},{2,3},{3,2},{4,5},{5,4},{6,7},{7,6},{8,9},{9,8},{10,11... | collective-permute-start | bytes 98312 | tf_op jit(solution)/shard_map/ppermute | solution.py:199
  9.2 2.2 %copy-start = (bf16[128,128,128]{2,1,0:T(8,128)(2,1)S(1)}, bf16[128,128,128]{2,1,0:T(8,128)(2,1)}, u32[]{:S(2)}) copy-start(bf16[128,128,128]{2,1,0:T(8,128)(2,1)} %density.1) | copy-start | bytes 12582916

commit v6 on v5

--- a/solution.py
+++ b/solution.py
@@ -9,6 +9,7 @@
 LOG2E = 1.4426950408889634
 CODE_TOP = 65535.0
 CODE_STEP = CODE_TOP / 24.0
+FACES_LIMIT = 53 * 1024 * 1024
 PREPARE_LIMIT = 24 * 1024 * 1024
 RENDER_LIMIT = 24 * 1024 * 1024
 
@@ -28,6 +29,53 @@
     for part in range(parts - 2, -1, -1):
         value = jnp.where(lane < (part + 1) * (rows // parts), occ[zb, part, xb], value)
     return value.astype(jnp.float32) * scale
+
+
+def faces_kernel(density, znear, zfar, xnear, xfar, planes_got, blocks_got, tiles, sems):
+    planes, columns, rows = density.shape
+    wanted = [
+        (density.at[0], planes_got.at[0]),
+        (density.at[planes - 1], planes_got.at[1]),
+        (density.at[:, pl.ds(0, BX), :], blocks_got.at[0]),
+        (density.at[:, pl.ds(columns - BX, BX), :], blocks_got.at[1]),
+    ]
+    copies = [pltpu.make_async_copy(a, b, sems.at[i]) for i, (a, b) in enumerate(wanted)]
+    for copy in copies:
+        copy.start()
+    for copy in copies:
+        copy.wait()
+
+    def face(side, row):
+        tiles[...] = blocks_got[side].astype(jnp.float32).reshape(planes * BX, rows)
+        return tiles[pl.ds(row, planes, stride=BX), :]
+
+    zpair = planes_got[0].astype(jnp.float32), planes_got[1].astype(jnp.float32)
+    xpair = face(0, 0), face(1, BX - 1)
+    for axis, (low, high), near, far in (
+        ("depth", zpair, znear, zfar), ("cols", xpair, xnear, xfar)
+    ):
+        odd = lax.rem(lax.axis_index(axis), 2) == 1
+        near[...] = jnp.where(odd, low, high).astype(near.dtype)
+        far[...] = jnp.where(odd, high, low).astype(far.dtype)
+
+
+def faces(density):
+    planes, columns, rows = density.shape
+    vmem = pl.BlockSpec(memory_space=pltpu.VMEM)
+    shapes = [(columns, rows)] * 2 + [(planes, rows)] * 2
+    return pl.pallas_call(
+        faces_kernel,
+        in_specs=[pl.BlockSpec(memory_space=pltpu.HBM)],
+        out_specs=[vmem] * 4,
+        out_shape=[jax.ShapeDtypeStruct(shape, density.dtype) for shape in shapes],
+        scratch_shapes=[
+            pltpu.VMEM((2, columns, rows), density.dtype),
+            pltpu.VMEM((2, planes, BX, rows), density.dtype),
+            pltpu.VMEM((planes * BX, rows), jnp.float32),
+            pltpu.SemaphoreType.DMA((4,)),
+        ],
+        compiler_params=pltpu.CompilerParams(vmem_limit_bytes=FACES_LIMIT),
+    )(density)
 
 
 def prepare_kernel(density, field, slope, diff):
@@ -146,7 +194,7 @@
 
     slabs, _, share, _ = out.shape
     for c in range(4):
-        turned = image[c].T
+        turned = encode((image[c] if c < 3 else -0.125 * image[c]).T)
         for d in range(slabs):
             out[d, c] = turned[d * share:(d + 1) * share, :]
 
@@ -160,7 +208,7 @@
         lambda *refs: render_kernel(depth_scale, *refs),
         in_specs=[smem] * 3 + [vmem] * 6,
         out_specs=vmem,
-        out_shape=jax.ShapeDtypeStruct((slabs, 4, rows // slabs, columns), jnp.float32),
+        out_shape=jax.ShapeDtypeStruct((slabs, 4, rows // slabs, columns), jnp.int16),
         scratch_shapes=[
             pltpu.VMEM((2, planes, rows), jnp.float32),
             pltpu.VMEM((4, columns, rows), jnp.float32),
@@ -171,11 +219,12 @@
 
 def composite(parts):
     slabs = parts.shape[0]
+    parts = decode(parts)
     colours, total = parts[slabs - 1, :3], parts[slabs - 1, 3:]
     for d in range(slabs - 2, -1, -1):
-        colours = colours + jnp.exp2(total) * parts[d, :3]
+        colours = colours + jnp.exp2(-8.0 * total) * parts[d, :3]
         total = total + parts[d, 3:]
-    return jnp.concatenate([colours, 1.0 - jnp.exp2(total)], axis=0)
+    return jnp.concatenate([colours, 1.0 - jnp.exp2(-8.0 * total)], axis=0)
 
 
 def encode(pixels):
@@ -190,13 +239,13 @@
     return jnp.where(code > -32768.0, jnp.exp2(level), 0.0)
 
 
-def neighbours(axis, low, high):
+def neighbours(axis, near, far):
     size = lax.axis_size(axis)
     odd = lax.axis_index(axis) % 2 == 1
-    near = [pair for i in range(0, size - 1, 2) for pair in ((i, i + 1), (i + 1, i))]
-    far = [pair for i in range(1, size - 1, 2) for pair in ((i, i + 1), (i + 1, i))]
-    from_far = lax.ppermute(jnp.where(odd, high, low), axis, far)
-    from_near = lax.ppermute(jnp.where(odd, low, high), axis, near)
+    evens = [pair for i in range(0, size - 1, 2) for pair in ((i, i + 1), (i + 1, i))]
+    odds = [pair for i in range(1, size - 1, 2) for pair in ((i, i + 1), (i + 1, i))]
+    from_far = lax.ppermute(far, axis, odds)
+    from_near = lax.ppermute(near, axis, evens)
     return jnp.where(odd, from_near, from_far), jnp.where(odd, from_far, from_near)
 
 
@@ -204,8 +253,9 @@
     planes, columns, rows = density.shape
     slabs = lax.axis_size("depth")
     devices = lax.axis_size("cols")
-    zhalo = neighbours("depth", density[0], density[-1])
-    xhalo = neighbours("cols", density[:, 0, :], density[:, -1, :])
+    znear, zfar, xnear, xfar = faces(density)
+    zhalo = neighbours("depth", znear, zfar)
+    xhalo = neighbours("cols", xnear, xfar)
     occ = occupancy.transpose(0, 2, 1)
     depth_scale = -3.0 / (planes * slabs)
     parts = render(prepare(density), occ, light_dir, palette.T, zhalo + xhalo, depth_scale, slabs)

time: 69.4 us -> 67 us (0.965)
  starting transfers between devices: 7.17 us -> 5.43 us
  Pallas kernels: 16 us -> 17.5 us
  local copies, waits for them, and re-layouts: 3.44 us -> 2.3 us
  other arithmetic: 2.28 us -> 1.56 us
    ppermute x4, starting transfers between devices: 7.17 us -> 5.43 us  [the longest x2 2.99 us: neighbours(): from_far = lax.ppermute(far, axis, odds)]
    pallas_call x0 -> x1, Pallas kernels: none -> 1.48 us  [faces(): pl.pallas_call(faces_kernel, in_specs=[pl.BlockSpec(memory_space=pltpu.HB...]
    slice x1 -> x0, local copies, waits for them, and re-layouts: 1.14 us -> none  [local(): xhalo = neighbours('cols', density[:, 0, :], density[:, -1, :])]
    all_to_all x1, blocking collectives: 28.5 us -> 27.5 us  [local(): codes = lax.all_to_all(codes, 'cols', 0, 0, tiled=True)]
    all_to_all x1, blocking collectives: 11.5 us -> 12.3 us  [local(): parts = lax.all_to_all(parts, 'depth', 0, 0, tiled=True)]
    select_n x2 -> x1, other arithmetic: 0.82 us -> 0.1 us  [decode(): return jnp.where(code > -32768.0, jnp.exp2(level), 0.0)]
  transfers between devices with their start and end apart: 4 -> 4, of which waited for: 0 -> 0; matrix products, arithmetic and copies ran while one was open for 2% -> 0% of each run, Pallas kernels for 3% -> 4%
where the time goes in v6:
time: 67 us; the launch traced here: 66.8 us
  blocking collectives  39.8 us (59%)
  Pallas kernels  17.5 us (26%)
  starting transfers between devices  5.43 us (8%)
  local copies, waits for them, and re-layouts  2.3 us (3%)
  other arithmetic  1.56 us (2%)
    all_to_all x1, blocking collectives, local(): codes = lax.all_to_all(codes, 'cols', 0, 0, tiled=True)  27.5 us
    pallas_call x1, Pallas kernels, render(): pl.pallas_call(lambda *refs: render_kernel(depth_scale, *refs), in_specs=...  13.6 us
    all_to_all x1, blocking collectives, local(): parts = lax.all_to_all(parts, 'depth', 0, 0, tiled=True)  12.3 us
    ppermute x2, starting transfers between devices, neighbours(): from_far = lax.ppermute(far, axis, odds)  2.99 us
    ppermute x2, starting transfers between devices, neighbours(): from_near = lax.ppermute(near, axis, evens)  2.44 us
    pallas_call x1, Pallas kernels, prepare(): pl.pallas_call(prepare_kernel, in_specs=[vmem], out_specs=[vmem] * 2, out...  2.36 us
    unnamed x8, local copies, waits for them, and re-layouts  2.19 us
    pallas_call x1, Pallas kernels, faces(): pl.pallas_call(faces_kernel, in_specs=[pl.BlockSpec(memory_space=pltpu.HB...  1.48 us
  transfers between devices with their start and end apart: 4, of which 0 were waited for; matrix products, arithmetic and copies ran while one was open for 0% of the time, Pallas kernels for 4%

profile of v6, /device:TPU:2, one launch (start us, length us, event | category | flops | bytes accessed | tf_op | source)
XLA Modules:
  0.0 66.8 jit_solution(22031935743114336)
XLA Ops:
  0.0 0.0 copy-start.2
  0.0 0.0 copy-start.3
  0.0 0.0 copy-start.1
  0.0 1.5 %shard_map.47 = (bf16[128,128]{1,0:T(8,128)(2,1)S(1)}, bf16[128,128]{1,0:T(8,128)(2,1)S(1)}, bf16[128,128]{1,0:T(8,128)(2,1)S(1)}, bf16[128,128]{1,0:T(8,128)(2,1)S(1)}) custom-call(bf16[128,128,128]{2,1,0:T(8,128)(2,1)} %density.3), custom_call_target="tpu_custom_call" | custom-call | tf_op jit(solution)/shard_map/pallas_call | solution.py:66
  1.5 0.1 collective-permute-start
  1.6 0.7 collective-permute-start.1
  2.3 2.3 %collective-permute-start.2 = (bf16[128,128]{1,0:T(8,128)(2,1)S(1)}, bf16[128,128]{1,0:T(8,128)(2,1)S(1)}, u32[]{:S(2)}, u32[]{:S(2)}) collective-permute-start(bf16[128,128]{1,0:T(8,128)(2,1)S(1)} %get-tuple-element.15), channel_id=1, source_target_pairs={{0,1},{1,0},{2,3},{3,2},{4,5},{5,4},{6,7},{7,6},{8,9},{9,8},{10,11... | collective-permute-start | bytes 98312 | tf_op jit(solution)/shard_map/ppermute | solution.py:248
  4.6 2.3 %collective-permute-start.3 = (bf16[128,128]{1,0:T(8,128)(2,1)S(1)}, bf16[128,128]{1,0:T(8,128)(2,1)S(1)}, u32[]{:S(2)}, u32[]{:S(2)}) collective-permute-start(bf16[128,128]{1,0:T(8,128)(2,1)S(1)} %get-tuple-element.16), channel_id=1, source_target_pairs={{1,2},{2,1},{3,4},{4,3},{5,6},{6,5},{7,8},{8,7},{9,10},{10,9},{11,... | collective-permute-start | bytes 98312 | tf_op jit(solution)/shard_map/ppermute | solution.py:247
  7.0 0.0 copy-start
  7.0 2.2 %copy-done = bf16[128,128,128]{2,1,0:T(8,128)(2,1)S(1)} copy-done((bf16[128,128,128]{2,1,0:T(8,128)(2,1)S(1)}, bf16[128,128,128]{2,1,0:T(8,128)(2,1)}, u32[]{:S(2)}) %copy-start) | copy-done | bytes 4194328
  9.2 2.4 %shard_map.46 = (f32[128,144,128]{2,1,0:T(8,128)S(1)}, f32[128,128,128]{2,1,0:T(8,128)S(1)}) custom-call(bf16[128,128,128]{2,1,0:T(8,128)(2,1)S(1)} %copy-done), custom_call_target="tpu_custom_call" | custom-call | flops 536870912 | bytes 20971520 | tf_op jit(solution)/shard_map/pallas_call | solution.py:98
  11.5 0.0 collective-permute-done
  11.5 0.0 collective-permute-done.1
  11.6 0.0 collective-permute-done.2
  11.6 0.0 collective-permute-done.3
  11.6 0.0 copy-done.2
  11.6 0.0 copy-done.3
  11.6 0.0 copy-done.1
  11.6 13.6 %shard_map.48 = s16[8,4,16,128]{3,2,1,0:T(8,128)(2,1)S(1)} custom-call(f32[3]{0:T(128)S(1)} %copy-done.3, f32[2,4]{1,0:T(2,128)S(1)} %bitcast.27, s32[8,4,8]{2,1,0:T(4,128)S(1)} %bitcast.26, f32[128,144,128]{2,1,0:T(8,128)S(1)} %get-tuple-element.11.refs_3_, f32[128,128,128]{2,1,0:T(8,128)S(1)} %get-tuple-element.12.refs_4_, ...), custom_call_target="tpu_custom_call" | custom-call | tf_op jit(solution)/shard_map/pallas_call | solution.py:207
  25.3 12.3 %all_to_all.10 = s16[8,4,16,128]{3,2,1,0:T(8,128)(2,1)S(1)} all-to-all(s16[8,4,16,128]{3,2,1,0:T(8,128)(2,1)S(1)} %shard_map.48), channel_id=1, replica_groups=mesh['depth'=8,'cols'=32] {'depth'}, dimensions={0} | all-to-all | bytes 262144 | tf_op jit(solution)/shard_map/all_to_all | solution.py:262
  37.6 0.1 fusion.8
  37.8 0.1 broadcast_in_dim.15
  37.9 27.5 %all_to_all.11 = s16[32,4,16,128]{3,2,1,0:T(8,128)(2,1)S(1)} all-to-all(s16[32,4,16,128]{3,2,1,0:T(8,128)(2,1)S(1)} %broadcast_in_dim.15), channel_id=1, replica_groups=mesh['depth'=8,'cols'=32] {'cols'}, dimensions={0} | all-to-all | bytes 1048576 | tf_op jit(solution)/shard_map/all_to_all | solution.py:265
  65.4 1.3 %copy_bitcast_fusion = f32[4,4096,16]{1,2,0:T(8,128)} fusion(s16[32,4,16,128]{3,2,1,0:T(8,128)(2,1)S(1)} %all_to_all.11), kind=kLoop, calls=%fused_computation.7 | loop fusion | flops 1572864 | bytes 1572864 | tf_op jit(solution)/shard_map/reshape | solution.py:266
  (7 shorter events, 0.1 us)
Async XLA Ops:
  0.0 11.6 %copy-start.2 = (f32[4,2]{0,1:T(2,128)S(1)}, f32[4,2]{0,1:T(2,128)}, u32[]{:S(2)}) copy-start(f32[4,2]{0,1:T(2,128)} %param.7) | copy-start | bytes 100
  0.0 11.6 %copy-start.3 = (f32[3]{0:T(128)S(1)}, f32[3]{0:T(128)}, u32[]{:S(2)}) copy-start(f32[3]{0:T(128)} %refs_0_.1) | copy-start | bytes 40
  0.0 11.6 %copy-start.1 = (s32[8,8,4]{1,2,0:T(4,128)S(1)}, s32[8,8,4]{1,2,0:T(4,128)}, u32[]{:S(2)}) copy-start(s32[8,8,4]{1,2,0:T(4,128)} %param.5) | copy-start | bytes 3076
  1.5 10.0 %collective-permute-start = (bf16[128,128]{1,0:T(8,128)(2,1)S(1)}, bf16[128,128]{1,0:T(8,128)(2,1)S(1)}, u32[]{:S(2)}, u32[]{:S(2)}) collective-permute-start(bf16[128,128]{1,0:T(8,128)(2,1)S(1)} %get-tuple-element.13), channel_id=1, source_target_pairs={{0,32},{32,0},{64,96},{96,64},{128,160},{160,128},{192,224},{224,1... | collective-permute-start | bytes 98312 | tf_op jit(solution)/shard_map/ppermute | solution.py:248
  1.6 9.9 %collective-permute-start.1 = (bf16[128,128]{1,0:T(8,128)(2,1)S(1)}, bf16[128,128]{1,0:T(8,128)(2,1)S(1)}, u32[]{:S(2)}, u32[]{:S(2)}) collective-permute-start(bf16[128,128]{1,0:T(8,128)(2,1)S(1)} %get-tuple-element.14), channel_id=1, source_target_pairs={{32,64},{64,32},{96,128},{128,96},{160,192},{192,160},{33,65},{65,... | collective-permute-start | bytes 98312 | tf_op jit(solution)/shard_map/ppermute | solution.py:247
  2.3 9.3 %collective-permute-start.2 = (bf16[128,128]{1,0:T(8,128)(2,1)S(1)}, bf16[128,128]{1,0:T(8,128)(2,1)S(1)}, u32[]{:S(2)}, u32[]{:S(2)}) collective-permute-start(bf16[128,128]{1,0:T(8,128)(2,1)S(1)} %get-tuple-element.15), channel_id=1, source_target_pairs={{0,1},{1,0},{2,3},{3,2},{4,5},{5,4},{6,7},{7,6},{8,9},{9,8},{10,11... | collective-permute-start | bytes 98312 | tf_op jit(solution)/shard_map/ppermute | solution.py:248
  4.6 7.0 %collective-permute-start.3 = (bf16[128,128]{1,0:T(8,128)(2,1)S(1)}, bf16[128,128]{1,0:T(8,128)(2,1)S(1)}, u32[]{:S(2)}, u32[]{:S(2)}) collective-permute-start(bf16[128,128]{1,0:T(8,128)(2,1)S(1)} %get-tuple-element.16), channel_id=1, source_target_pairs={{1,2},{2,1},{3,4},{4,3},{5,6},{6,5},{7,8},{8,7},{9,10},{10,9},{11,... | collective-permute-start | bytes 98312 | tf_op jit(solution)/shard_map/ppermute | solution.py:247
  7.0 2.2 %copy-start = (bf16[128,128,128]{2,1,0:T(8,128)(2,1)S(1)}, bf16[128,128,128]{2,1,0:T(8,128)(2,1)}, u32[]{:S(2)}) copy-start(bf16[128,128,128]{2,1,0:T(8,128)(2,1)} %density.3) | copy-start | bytes 12582916

commit v7 on v6

--- a/solution.py
+++ b/solution.py
@@ -82,14 +82,14 @@
     planes, columns, rows = density.shape
     diff[...] = difference_matrix(rows)
 
-    @pl.loop(0, planes // 16)
+    @pl.loop(0, planes // 64)
     def _(k):
-        at = pl.ds(16 * k, 16)
+        at = pl.ds(64 * k, 64)
         part = density[at]
         field[at, 8:8 + columns, :] = part.astype(jnp.float32)
-        step = jnp.dot(part.reshape(16 * columns, rows), diff[...],
+        step = jnp.dot(part.reshape(64 * columns, rows), diff[...],
                        preferred_element_type=jnp.float32)
-        slope[at] = step.reshape(16, columns, rows)
+        slope[at] = step.reshape(64, columns, rows)
 
 
 def prepare(density):

time: 67 us -> 66.8 us (level)
  Pallas kernels: 17.5 us -> 16.5 us
  blocking collectives: 39.8 us -> 40.5 us
    pallas_call x1, Pallas kernels: 2.36 us -> 1.43 us  [prepare(): pl.pallas_call(prepare_kernel, in_specs=[vmem], out_specs=[vmem] * 2, out...]
    all_to_all x1, blocking collectives: 27.5 us -> 28.2 us  [local(): codes = lax.all_to_all(codes, 'cols', 0, 0, tiled=True)]
  transfers between devices with their start and end apart: 4 -> 4, of which waited for: 0 -> 0; matrix products, arithmetic and copies ran while one was open for 0% -> 0% of each run, Pallas kernels for 4% -> 2%
where the time goes in v7:
time: 66.8 us; the launch traced here: 66.6 us
  blocking collectives  40.5 us (61%)
  Pallas kernels  16.5 us (25%)
  starting transfers between devices  5.43 us (8%)
  local copies, waits for them, and re-layouts  2.3 us (3%)
  other arithmetic  1.56 us (2%)
    all_to_all x1, blocking collectives, local(): codes = lax.all_to_all(codes, 'cols', 0, 0, tiled=True)  28.2 us
    pallas_call x1, Pallas kernels, render(): pl.pallas_call(lambda *refs: render_kernel(depth_scale, *refs), in_specs=...  13.6 us
    all_to_all x1, blocking collectives, local(): parts = lax.all_to_all(parts, 'depth', 0, 0, tiled=True)  12.3 us
    ppermute x2, starting transfers between devices, neighbours(): from_far = lax.ppermute(far, axis, odds)  2.99 us
    ppermute x2, starting transfers between devices, neighbours(): from_near = lax.ppermute(near, axis, evens)  2.44 us
    unnamed x8, local copies, waits for them, and re-layouts  2.19 us
    pallas_call x1, Pallas kernels, faces(): pl.pallas_call(faces_kernel, in_specs=[pl.BlockSpec(memory_space=pltpu.HB...  1.48 us
    pallas_call x1, Pallas kernels, prepare(): pl.pallas_call(prepare_kernel, in_specs=[vmem], out_specs=[vmem] * 2, out...  1.43 us
  transfers between devices with their start and end apart: 4, of which 0 were waited for; matrix products, arithmetic and copies ran while one was open for 0% of the time, Pallas kernels for 2%

profile of v7, /device:TPU:2, one launch (start us, length us, event | category | flops | bytes accessed | tf_op | source)
XLA Modules:
  0.0 66.6 jit_solution(12592339025306342460)
XLA Ops:
  0.0 0.0 copy-start.2
  0.0 0.0 copy-start.3
  0.0 0.0 copy-start.1
  0.0 1.5 %shard_map.47 = (bf16[128,128]{1,0:T(8,128)(2,1)S(1)}, bf16[128,128]{1,0:T(8,128)(2,1)S(1)}, bf16[128,128]{1,0:T(8,128)(2,1)S(1)}, bf16[128,128]{1,0:T(8,128)(2,1)S(1)}) custom-call(bf16[128,128,128]{2,1,0:T(8,128)(2,1)} %density.3), custom_call_target="tpu_custom_call" | custom-call | tf_op jit(solution)/shard_map/pallas_call | solution.py:66
  1.5 0.1 collective-permute-start
  1.6 0.7 collective-permute-start.1
  2.3 2.3 %collective-permute-start.2 = (bf16[128,128]{1,0:T(8,128)(2,1)S(1)}, bf16[128,128]{1,0:T(8,128)(2,1)S(1)}, u32[]{:S(2)}, u32[]{:S(2)}) collective-permute-start(bf16[128,128]{1,0:T(8,128)(2,1)S(1)} %get-tuple-element.15), channel_id=1, source_target_pairs={{0,1},{1,0},{2,3},{3,2},{4,5},{5,4},{6,7},{7,6},{8,9},{9,8},{10,11... | collective-permute-start | bytes 98312 | tf_op jit(solution)/shard_map/ppermute | solution.py:248
  4.6 2.3 %collective-permute-start.3 = (bf16[128,128]{1,0:T(8,128)(2,1)S(1)}, bf16[128,128]{1,0:T(8,128)(2,1)S(1)}, u32[]{:S(2)}, u32[]{:S(2)}) collective-permute-start(bf16[128,128]{1,0:T(8,128)(2,1)S(1)} %get-tuple-element.16), channel_id=1, source_target_pairs={{1,2},{2,1},{3,4},{4,3},{5,6},{6,5},{7,8},{8,7},{9,10},{10,9},{11,... | collective-permute-start | bytes 98312 | tf_op jit(solution)/shard_map/ppermute | solution.py:247
  7.0 0.0 copy-start
  7.0 2.2 %copy-done = bf16[128,128,128]{2,1,0:T(8,128)(2,1)S(1)} copy-done((bf16[128,128,128]{2,1,0:T(8,128)(2,1)S(1)}, bf16[128,128,128]{2,1,0:T(8,128)(2,1)}, u32[]{:S(2)}) %copy-start) | copy-done | bytes 4194328
  9.2 1.4 %shard_map.46 = (f32[128,144,128]{2,1,0:T(8,128)S(1)}, f32[128,128,128]{2,1,0:T(8,128)S(1)}) custom-call(bf16[128,128,128]{2,1,0:T(8,128)(2,1)S(1)} %copy-done), custom_call_target="tpu_custom_call" | custom-call | flops 536870912 | bytes 20971520 | tf_op jit(solution)/shard_map/pallas_call | solution.py:98
  10.6 0.0 collective-permute-done
  10.6 0.0 collective-permute-done.1
  10.6 0.0 collective-permute-done.2
  10.7 0.0 collective-permute-done.3
  10.7 0.0 copy-done.2
  10.7 0.0 copy-done.3
  10.7 0.0 copy-done.1
  10.7 13.6 %shard_map.48 = s16[8,4,16,128]{3,2,1,0:T(8,128)(2,1)S(1)} custom-call(f32[3]{0:T(128)S(1)} %copy-done.3, f32[2,4]{1,0:T(2,128)S(1)} %bitcast.27, s32[8,4,8]{2,1,0:T(4,128)S(1)} %bitcast.26, f32[128,144,128]{2,1,0:T(8,128)S(1)} %get-tuple-element.11.refs_3_, f32[128,128,128]{2,1,0:T(8,128)S(1)} %get-tuple-element.12.refs_4_, ...), custom_call_target="tpu_custom_call" | custom-call | tf_op jit(solution)/shard_map/pallas_call | solution.py:207
  24.3 12.3 %all_to_all.10 = s16[8,4,16,128]{3,2,1,0:T(8,128)(2,1)S(1)} all-to-all(s16[8,4,16,128]{3,2,1,0:T(8,128)(2,1)S(1)} %shard_map.48), channel_id=1, replica_groups=mesh['depth'=8,'cols'=32] {'depth'}, dimensions={0} | all-to-all | bytes 262144 | tf_op jit(solution)/shard_map/all_to_all | solution.py:262
  36.6 0.1 fusion.8
  36.9 0.1 broadcast_in_dim.15
  37.0 28.2 %all_to_all.11 = s16[32,4,16,128]{3,2,1,0:T(8,128)(2,1)S(1)} all-to-all(s16[32,4,16,128]{3,2,1,0:T(8,128)(2,1)S(1)} %broadcast_in_dim.15), channel_id=1, replica_groups=mesh['depth'=8,'cols'=32] {'cols'}, dimensions={0} | all-to-all | bytes 1048576 | tf_op jit(solution)/shard_map/all_to_all | solution.py:265
  65.2 1.3 %copy_bitcast_fusion = f32[4,4096,16]{1,2,0:T(8,128)} fusion(s16[32,4,16,128]{3,2,1,0:T(8,128)(2,1)S(1)} %all_to_all.11), kind=kLoop, calls=%fused_computation.7 | loop fusion | flops 1572864 | bytes 1572864 | tf_op jit(solution)/shard_map/reshape | solution.py:266
  (7 shorter events, 0.1 us)
Async XLA Ops:
  0.0 10.7 %copy-start.2 = (f32[4,2]{0,1:T(2,128)S(1)}, f32[4,2]{0,1:T(2,128)}, u32[]{:S(2)}) copy-start(f32[4,2]{0,1:T(2,128)} %param.7) | copy-start | bytes 100
  0.0 10.7 %copy-start.3 = (f32[3]{0:T(128)S(1)}, f32[3]{0:T(128)}, u32[]{:S(2)}) copy-start(f32[3]{0:T(128)} %refs_0_.1) | copy-start | bytes 40
  0.0 10.7 %copy-start.1 = (s32[8,8,4]{1,2,0:T(4,128)S(1)}, s32[8,8,4]{1,2,0:T(4,128)}, u32[]{:S(2)}) copy-start(s32[8,8,4]{1,2,0:T(4,128)} %param.5) | copy-start | bytes 3076
  1.5 9.1 %collective-permute-start = (bf16[128,128]{1,0:T(8,128)(2,1)S(1)}, bf16[128,128]{1,0:T(8,128)(2,1)S(1)}, u32[]{:S(2)}, u32[]{:S(2)}) collective-permute-start(bf16[128,128]{1,0:T(8,128)(2,1)S(1)} %get-tuple-element.13), channel_id=1, source_target_pairs={{0,32},{32,0},{64,96},{96,64},{128,160},{160,128},{192,224},{224,1... | collective-permute-start | bytes 98312 | tf_op jit(solution)/shard_map/ppermute | solution.py:248
  1.6 9.0 %collective-permute-start.1 = (bf16[128,128]{1,0:T(8,128)(2,1)S(1)}, bf16[128,128]{1,0:T(8,128)(2,1)S(1)}, u32[]{:S(2)}, u32[]{:S(2)}) collective-permute-start(bf16[128,128]{1,0:T(8,128)(2,1)S(1)} %get-tuple-element.14), channel_id=1, source_target_pairs={{32,64},{64,32},{96,128},{128,96},{160,192},{192,160},{33,65},{65,... | collective-permute-start | bytes 98312 | tf_op jit(solution)/shard_map/ppermute | solution.py:247
  2.3 8.4 %collective-permute-start.2 = (bf16[128,128]{1,0:T(8,128)(2,1)S(1)}, bf16[128,128]{1,0:T(8,128)(2,1)S(1)}, u32[]{:S(2)}, u32[]{:S(2)}) collective-permute-start(bf16[128,128]{1,0:T(8,128)(2,1)S(1)} %get-tuple-element.15), channel_id=1, source_target_pairs={{0,1},{1,0},{2,3},{3,2},{4,5},{5,4},{6,7},{7,6},{8,9},{9,8},{10,11... | collective-permute-start | bytes 98312 | tf_op jit(solution)/shard_map/ppermute | solution.py:248
  4.6 6.0 %collective-permute-start.3 = (bf16[128,128]{1,0:T(8,128)(2,1)S(1)}, bf16[128,128]{1,0:T(8,128)(2,1)S(1)}, u32[]{:S(2)}, u32[]{:S(2)}) collective-permute-start(bf16[128,128]{1,0:T(8,128)(2,1)S(1)} %get-tuple-element.16), channel_id=1, source_target_pairs={{1,2},{2,1},{3,4},{4,3},{5,6},{6,5},{7,8},{8,7},{9,10},{10,9},{11,... | collective-permute-start | bytes 98312 | tf_op jit(solution)/shard_map/ppermute | solution.py:247
  7.0 2.2 %copy-start = (bf16[128,128,128]{2,1,0:T(8,128)(2,1)S(1)}, bf16[128,128,128]{2,1,0:T(8,128)(2,1)}, u32[]{:S(2)}) copy-start(bf16[128,128,128]{2,1,0:T(8,128)(2,1)} %density.3) | copy-start | bytes 12582916

commit v8 on v7

--- a/solution.py
+++ b/solution.py
@@ -46,7 +46,8 @@
         copy.wait()
 
     def face(side, row):
-        tiles[...] = blocks_got[side].astype(jnp.float32).reshape(planes * BX, rows)
+        block = blocks_got[side].astype(jnp.float32)
+        tiles[0:planes * BX, :] = block.reshape(planes * BX, rows)
         return tiles[pl.ds(row, planes, stride=BX), :]
 
     zpair = planes_got[0].astype(jnp.float32), planes_got[1].astype(jnp.float32)
@@ -71,7 +72,7 @@
         scratch_shapes=[
             pltpu.VMEM((2, columns, rows), density.dtype),
             pltpu.VMEM((2, planes, BX, rows), density.dtype),
-            pltpu.VMEM((planes * BX, rows), jnp.float32),
+            pltpu.VMEM(((planes + 1) * BX, rows), jnp.float32),
             pltpu.SemaphoreType.DMA((4,)),
         ],
         compiler_params=pltpu.CompilerParams(vmem_limit_bytes=FACES_LIMIT),

time: 66.8 us -> 66.8 us (level)
  no operation moved by 1% of the time
where the time goes in v8:
time: 66.8 us; the launch traced here: 66.6 us
  blocking collectives  40.5 us (61%)
  Pallas kernels  16.5 us (25%)
  starting transfers between devices  5.43 us (8%)
  local copies, waits for them, and re-layouts  2.3 us (3%)
  other arithmetic  1.56 us (2%)
    all_to_all x1, blocking collectives, local(): codes = lax.all_to_all(codes, 'cols', 0, 0, tiled=True)  28.2 us
    pallas_call x1, Pallas kernels, render(): pl.pallas_call(lambda *refs: render_kernel(depth_scale, *refs), in_specs=...  13.6 us
    all_to_all x1, blocking collectives, local(): parts = lax.all_to_all(parts, 'depth', 0, 0, tiled=True)  12.3 us
    ppermute x2, starting transfers between devices, neighbours(): from_far = lax.ppermute(far, axis, odds)  2.99 us
    ppermute x2, starting transfers between devices, neighbours(): from_near = lax.ppermute(near, axis, evens)  2.44 us
    unnamed x8, local copies, waits for them, and re-layouts  2.19 us
    pallas_call x1, Pallas kernels, faces(): pl.pallas_call(faces_kernel, in_specs=[pl.BlockSpec(memory_space=pltpu.HB...  1.48 us
    pallas_call x1, Pallas kernels, prepare(): pl.pallas_call(prepare_kernel, in_specs=[vmem], out_specs=[vmem] * 2, out...  1.43 us
  transfers between devices with their start and end apart: 4, of which 0 were waited for; matrix products, arithmetic and copies ran while one was open for 0% of the time, Pallas kernels for 2%

profile of v8, /device:TPU:2, one launch (start us, length us, event | category | flops | bytes accessed | tf_op | source)
XLA Modules:
  0.0 66.6 jit_solution(12423774478119350005)
XLA Ops:
  0.0 0.0 copy-start.2
  0.0 0.0 copy-start.3
  0.0 0.0 copy-start.1
  0.0 1.5 %shard_map.47 = (bf16[128,128]{1,0:T(8,128)(2,1)S(1)}, bf16[128,128]{1,0:T(8,128)(2,1)S(1)}, bf16[128,128]{1,0:T(8,128)(2,1)S(1)}, bf16[128,128]{1,0:T(8,128)(2,1)S(1)}) custom-call(bf16[128,128,128]{2,1,0:T(8,128)(2,1)} %density.3), custom_call_target="tpu_custom_call" | custom-call | tf_op jit(solution)/shard_map/pallas_call | solution.py:67
  1.5 0.1 collective-permute-start
  1.6 0.7 collective-permute-start.1
  2.3 2.3 %collective-permute-start.2 = (bf16[128,128]{1,0:T(8,128)(2,1)S(1)}, bf16[128,128]{1,0:T(8,128)(2,1)S(1)}, u32[]{:S(2)}, u32[]{:S(2)}) collective-permute-start(bf16[128,128]{1,0:T(8,128)(2,1)S(1)} %get-tuple-element.15), channel_id=1, source_target_pairs={{0,1},{1,0},{2,3},{3,2},{4,5},{5,4},{6,7},{7,6},{8,9},{9,8},{10,11... | collective-permute-start | bytes 98312 | tf_op jit(solution)/shard_map/ppermute | solution.py:249
  4.6 2.3 %collective-permute-start.3 = (bf16[128,128]{1,0:T(8,128)(2,1)S(1)}, bf16[128,128]{1,0:T(8,128)(2,1)S(1)}, u32[]{:S(2)}, u32[]{:S(2)}) collective-permute-start(bf16[128,128]{1,0:T(8,128)(2,1)S(1)} %get-tuple-element.16), channel_id=1, source_target_pairs={{1,2},{2,1},{3,4},{4,3},{5,6},{6,5},{7,8},{8,7},{9,10},{10,9},{11,... | collective-permute-start | bytes 98312 | tf_op jit(solution)/shard_map/ppermute | solution.py:248
  7.0 0.0 copy-start
  7.0 2.2 %copy-done = bf16[128,128,128]{2,1,0:T(8,128)(2,1)S(1)} copy-done((bf16[128,128,128]{2,1,0:T(8,128)(2,1)S(1)}, bf16[128,128,128]{2,1,0:T(8,128)(2,1)}, u32[]{:S(2)}) %copy-start) | copy-done | bytes 4194328
  9.2 1.4 %shard_map.46 = (f32[128,144,128]{2,1,0:T(8,128)S(1)}, f32[128,128,128]{2,1,0:T(8,128)S(1)}) custom-call(bf16[128,128,128]{2,1,0:T(8,128)(2,1)S(1)} %copy-done), custom_call_target="tpu_custom_call" | custom-call | flops 536870912 | bytes 20971520 | tf_op jit(solution)/shard_map/pallas_call | solution.py:99
  10.6 0.0 collective-permute-done
  10.6 0.0 collective-permute-done.1
  10.6 0.0 collective-permute-done.2
  10.6 0.0 collective-permute-done.3
  10.7 0.0 copy-done.2
  10.7 0.0 copy-done.3
  10.7 0.0 copy-done.1
  10.7 13.6 %shard_map.48 = s16[8,4,16,128]{3,2,1,0:T(8,128)(2,1)S(1)} custom-call(f32[3]{0:T(128)S(1)} %copy-done.3, f32[2,4]{1,0:T(2,128)S(1)} %bitcast.27, s32[8,4,8]{2,1,0:T(4,128)S(1)} %bitcast.26, f32[128,144,128]{2,1,0:T(8,128)S(1)} %get-tuple-element.11.refs_3_, f32[128,128,128]{2,1,0:T(8,128)S(1)} %get-tuple-element.12.refs_4_, ...), custom_call_target="tpu_custom_call" | custom-call | tf_op jit(solution)/shard_map/pallas_call | solution.py:208
  24.3 12.3 %all_to_all.10 = s16[8,4,16,128]{3,2,1,0:T(8,128)(2,1)S(1)} all-to-all(s16[8,4,16,128]{3,2,1,0:T(8,128)(2,1)S(1)} %shard_map.48), channel_id=1, replica_groups=mesh['depth'=8,'cols'=32] {'depth'}, dimensions={0} | all-to-all | bytes 262144 | tf_op jit(solution)/shard_map/all_to_all | solution.py:263
  36.6 0.1 fusion.8
  36.9 0.1 broadcast_in_dim.15
  37.0 28.2 %all_to_all.11 = s16[32,4,16,128]{3,2,1,0:T(8,128)(2,1)S(1)} all-to-all(s16[32,4,16,128]{3,2,1,0:T(8,128)(2,1)S(1)} %broadcast_in_dim.15), channel_id=1, replica_groups=mesh['depth'=8,'cols'=32] {'cols'}, dimensions={0} | all-to-all | bytes 1048576 | tf_op jit(solution)/shard_map/all_to_all | solution.py:266
  65.2 1.3 %copy_bitcast_fusion = f32[4,4096,16]{1,2,0:T(8,128)} fusion(s16[32,4,16,128]{3,2,1,0:T(8,128)(2,1)S(1)} %all_to_all.11), kind=kLoop, calls=%fused_computation.7 | loop fusion | flops 1572864 | bytes 1572864 | tf_op jit(solution)/shard_map/reshape | solution.py:267
  (7 shorter events, 0.1 us)
Async XLA Ops:
  0.0 10.7 %copy-start.2 = (f32[4,2]{0,1:T(2,128)S(1)}, f32[4,2]{0,1:T(2,128)}, u32[]{:S(2)}) copy-start(f32[4,2]{0,1:T(2,128)} %param.7) | copy-start | bytes 100
  0.0 10.7 %copy-start.3 = (f32[3]{0:T(128)S(1)}, f32[3]{0:T(128)}, u32[]{:S(2)}) copy-start(f32[3]{0:T(128)} %refs_0_.1) | copy-start | bytes 40
  0.0 10.7 %copy-start.1 = (s32[8,8,4]{1,2,0:T(4,128)S(1)}, s32[8,8,4]{1,2,0:T(4,128)}, u32[]{:S(2)}) copy-start(s32[8,8,4]{1,2,0:T(4,128)} %param.5) | copy-start | bytes 3076
  1.5 9.1 %collective-permute-start = (bf16[128,128]{1,0:T(8,128)(2,1)S(1)}, bf16[128,128]{1,0:T(8,128)(2,1)S(1)}, u32[]{:S(2)}, u32[]{:S(2)}) collective-permute-start(bf16[128,128]{1,0:T(8,128)(2,1)S(1)} %get-tuple-element.13), channel_id=1, source_target_pairs={{0,32},{32,0},{64,96},{96,64},{128,160},{160,128},{192,224},{224,1... | collective-permute-start | bytes 98312 | tf_op jit(solution)/shard_map/ppermute | solution.py:249
  1.6 9.0 %collective-permute-start.1 = (bf16[128,128]{1,0:T(8,128)(2,1)S(1)}, bf16[128,128]{1,0:T(8,128)(2,1)S(1)}, u32[]{:S(2)}, u32[]{:S(2)}) collective-permute-start(bf16[128,128]{1,0:T(8,128)(2,1)S(1)} %get-tuple-element.14), channel_id=1, source_target_pairs={{32,64},{64,32},{96,128},{128,96},{160,192},{192,160},{33,65},{65,... | collective-permute-start | bytes 98312 | tf_op jit(solution)/shard_map/ppermute | solution.py:248
  2.3 8.4 %collective-permute-start.2 = (bf16[128,128]{1,0:T(8,128)(2,1)S(1)}, bf16[128,128]{1,0:T(8,128)(2,1)S(1)}, u32[]{:S(2)}, u32[]{:S(2)}) collective-permute-start(bf16[128,128]{1,0:T(8,128)(2,1)S(1)} %get-tuple-element.15), channel_id=1, source_target_pairs={{0,1},{1,0},{2,3},{3,2},{4,5},{5,4},{6,7},{7,6},{8,9},{9,8},{10,11... | collective-permute-start | bytes 98312 | tf_op jit(solution)/shard_map/ppermute | solution.py:249
  4.6 6.0 %collective-permute-start.3 = (bf16[128,128]{1,0:T(8,128)(2,1)S(1)}, bf16[128,128]{1,0:T(8,128)(2,1)S(1)}, u32[]{:S(2)}, u32[]{:S(2)}) collective-permute-start(bf16[128,128]{1,0:T(8,128)(2,1)S(1)} %get-tuple-element.16), channel_id=1, source_target_pairs={{1,2},{2,1},{3,4},{4,3},{5,6},{6,5},{7,8},{8,7},{9,10},{10,9},{11,... | collective-permute-start | bytes 98312 | tf_op jit(solution)/shard_map/ppermute | solution.py:248
  7.0 2.2 %copy-start = (bf16[128,128,128]{2,1,0:T(8,128)(2,1)S(1)}, bf16[128,128,128]{2,1,0:T(8,128)(2,1)}, u32[]{:S(2)}) copy-start(bf16[128,128,128]{2,1,0:T(8,128)(2,1)} %density.3) | copy-start | bytes 12582916
